TPU v7x, 512 devices: a whole 4x4x16 slice. The times are simulated.
512 devices in a mesh: scene: 64 (over z_lo, x, core), tile: 8 (over z_hi, y).
Axes of the slice: x: 4, y: 4, z: 16 (z_hi: 2, z_lo: 8; z = z_hi * 8 + z_lo), core: 2. Of those that a mesh axis runs over, the one named last changes fastest.
Arguments:
- radiance: bfloat16 [512, 8, 10, 8192], P(('scene', 'tile')), may hold values from -8 to 8
- cloud_weight: int32 [512, 8, 8192], P(('scene', 'tile')), may hold values from 0 to 15
- footprint: int32 [512, 8], replicated, may hold values from 0 to 63, as said below
Outputs:
- composite: bfloat16 [64, 10, 8192], P('tile', None, 'scene')
- overview_one: bfloat16 [64, 10, 64, 32], P('tile')
- overview_two: bfloat16 [64, 10, 32, 16], P('tile')
- overview_three: bfloat16 [64, 10, 16, 8], P('tile')
- overview_four: bfloat16 [64, 10, 8, 4], P('tile')
- overview_five: bfloat16 [64, 10, 4, 2], P('tile')
Inputs may be any that keep to these rules, and one draw needn't show every extreme that they name: `footprint`: each row names 8 different tiles; at most 2 tiles of a row share the value of tile // 8, and in every row some such group holds exactly 2 tiles.
All inputs are finite; a program needn't handle non-finite values.
Results may differ from a plain program's by a relative error of at most 0.012.
Values may be sent and summed in bfloat16 or wider, within the bound.
A program may use at most 128 MiB of HBM per device.

v0:
```python
import jax
import jax.numpy as jnp
from jax import lax
from jax.sharding import PartitionSpec as P

K = 8
TILE_DEV = 8
COLS = 64


def average_pool(values):
    height = values.shape[-2]
    width = values.shape[-1]
    shaped = values.astype(jnp.float32).reshape(values.shape[:-2] + (height // 2, 2, width // 2, 2))
    return jnp.mean(shaped, axis=(-3, -1)).astype(jnp.bfloat16)


def owner_rank(tile_rows, tile_dev):
    owner_of = tile_rows // tile_dev
    same_owner = owner_of[..., :, None] == owner_of[..., None, :]
    positions = jnp.arange(tile_rows.shape[-1])
    earlier = positions[None, :] < positions[:, None]
    rank_of = jnp.sum(jnp.logical_and(same_owner, earlier), axis=-1)
    return (owner_of, rank_of)


def slot_table(tile_rows, owner_index, capacity, tile_dev):
    owner_of, rank_of = owner_rank(tile_rows, tile_dev)
    matched = owner_of == owner_index
    local_tile = tile_rows - owner_index * tile_dev
    by_rank = jnp.logical_and(
        matched[..., None], rank_of[..., None] == jnp.arange(capacity)
    ).astype(jnp.float32)
    by_tile = (local_tile[..., None] == jnp.arange(tile_dev)).astype(jnp.float32)
    return jnp.einsum("skc,sku->scu", by_rank, by_tile, precision=lax.Precision.HIGHEST)


def on_device(radiance, cloud_weight, footprint):
    owners = lax.axis_size("tile")
    capacity = max(2, 2 * K // owners)
    scene_index = lax.axis_index("scene")
    tile_index = lax.axis_index("tile")
    device = scene_index * owners + tile_index
    pixels = radiance.shape[3]
    bands = radiance.shape[2]
    my_row = lax.dynamic_slice_in_dim(footprint, device, 1, 0)[0]
    owner_of, rank_of = owner_rank(my_row, TILE_DEV)
    slot_of = owner_of * capacity + rank_of
    placement = (jnp.arange(owners * capacity)[:, None] == slot_of[None, :]).astype(jnp.bfloat16)
    send_rad = jnp.einsum("pk,kbq->pbq", placement, radiance[0], preferred_element_type=jnp.float32)
    send_rad = send_rad.astype(jnp.bfloat16).reshape(owners, capacity, bands, pixels)
    weight_bf = cloud_weight[0].astype(jnp.bfloat16)
    send_weight = jnp.dot(placement, weight_bf, preferred_element_type=jnp.float32)
    send_weight = send_weight.astype(jnp.bfloat16).reshape(owners, capacity, 1, pixels)
    got_rad, got_weight = (
        lax.all_to_all(send_rad, "tile", split_axis=0, concat_axis=0, tiled=True),
        lax.all_to_all(send_weight, "tile", split_axis=0, concat_axis=0, tiled=True),
    )
    source_rows = lax.dynamic_slice_in_dim(footprint, scene_index * owners, owners, 0)
    assign = slot_table(source_rows, tile_index, capacity, TILE_DEV)
    weight_float = got_weight[:, :, 0, :].astype(jnp.float32)
    product = weight_float[:, :, None, :] * got_rad.astype(jnp.float32)
    local_sums = jnp.einsum("scu,scbq->ubq", assign, product, precision=lax.Precision.HIGHEST)
    local_totals = jnp.einsum("scu,scq->uq", assign, weight_float, precision=lax.Precision.HIGHEST)
    weighted_sums, weight_totals = (
        lax.psum_scatter(local_sums, "scene", scatter_dimension=2, tiled=True),
        lax.psum_scatter(local_totals, "scene", scatter_dimension=1, tiled=True),
    )
    composite = (weighted_sums / jnp.maximum(weight_totals, 1.0)[:, None, :]).astype(jnp.bfloat16)
    local_rows = composite.shape[2] // COLS
    grid = composite.reshape(composite.shape[0], bands, local_rows, COLS)
    whole_grid = lax.all_gather(grid, "scene", axis=2, tiled=True)
    overview_one = average_pool(whole_grid)
    overview_two = average_pool(overview_one)
    overview_three = average_pool(overview_two)
    overview_four = average_pool(overview_three)
    overview_five = average_pool(overview_four)
    return (composite, overview_one, overview_two, overview_three, overview_four, overview_five)


def solution(mesh):
    in_specs = (P(("scene", "tile"), None, None, None), P(("scene", "tile"), None, None), P())
    out_specs = (
        P("tile", None, "scene"),
        P("tile", None, None, None),
        P("tile", None, None, None),
        P("tile", None, None, None),
        P("tile", None, None, None),
        P("tile", None, None, None),
    )
    return jax.shard_map(
        on_device, mesh=mesh, in_specs=in_specs, out_specs=out_specs, check_vma=False
    )
```

profile of v0, /device:TPU:1, one launch (start us, length us, event | category | flops | bytes accessed | tf_op | source)
XLA Modules:
  0.0 1196.3 jit_solution(4927155921936412516)
XLA Ops:
  7.2 0.0 copy-start
  7.2 0.9 constant_dynamic-slice_fusion
  8.1 0.1 copy.108
  8.2 0.2 convert_reduce_fusion.5
  8.4 1.3 convolution_convert_fusion.1
  9.7 0.9 reshape.103
  10.5 18.3 %all-to-all-start = ((bf16[8,2,1,8192]{3,1,2,0:T(2,128)(2,1)}), bf16[8,2,1,8192]{3,1,2,0:T(2,128)(2,1)S(1)}, u32[]{:S(2)}, u32[]{:S(2)}) async-start(bf16[8,2,1,8192]{3,1,2,0:T(2,128)(2,1)} %bitcast.6), calls=%async_computation | async-start | bytes 524288 | tf_op jit(solution)/shard_map/all_to_all | solution.py:57
  28.8 0.0 copy-done
  28.8 2.4 convolution_convert_fusion
  31.2 5.4 reshape.104
  36.5 7.5 copy.94
  44.0 0.0 copy-start.3
  44.0 0.1 all-to-all-done
  44.1 13.9 %all-to-all-start.1 = ((bf16[8,2,10,8192]{3,1,2,0:T(2,128)(2,1)}), bf16[8,2,10,8192]{3,1,2,0:T(2,128)(2,1)}, u32[]{:S(2)}, u32[]{:S(2)}) async-start(bf16[8,2,10,8192]{3,1,2,0:T(2,128)(2,1)} %copy.94), calls=%async_computation.1 | async-start | bytes 5242880 | tf_op jit(solution)/shard_map/all_to_all | solution.py:56
  58.0 0.0 reduce-scatter.5.cloned.1.call-start
  58.0 0.0 copy-done.3
  58.0 0.1 dynamic-slice_subtract_fusion
  58.1 0.1 copy.90
  58.2 0.1 broadcast_compare_fusion
  58.3 0.1 copy.87
  58.4 0.1 copy.88
  58.4 0.3 convert_reduce_fusion.4
  58.7 0.2 fusion.9
  58.9 0.1 copy.96
  59.0 1.1 convolution_bitcast_fusion.1
  60.1 0.0 reduce-scatter.5.cloned.1.call-update
  60.1 0.0 reduce-scatter.3.cloned.1.call-start
  60.1 0.2 bitcast_convert_fusion
  60.3 47.7 %all-to-all-done.1 = bf16[8,2,10,8192]{3,1,2,0:T(2,128)(2,1)} async-done(((bf16[8,2,10,8192]{3,1,2,0:T(2,128)(2,1)}), bf16[8,2,10,8192]{3,1,2,0:T(2,128)(2,1)}, u32[]{:S(2)}, u32[]{:S(2)}) %all-to-all-start.1) | async-done | bytes 2621472 | tf_op jit(solution)/shard_map/all_to_all | solution.py:56
  108.0 7.3 convolution_bitcast_fusion
  115.3 0.0 reduce-scatter.3.cloned.1.call-update
  115.3 0.2 all-gather.2.cloned.1.call-start
  115.5 429.0 %reduce-scatter.5.cloned.1.call-done = f32[8,128]{1,0:T(8,128)} async-done(((f32[8,8192]{1,0:T(8,128)}), f32[8,128]{1,0:T(8,128)}) %reduce-scatter.5.cloned.1.call-update) | async-done | bytes 4112 | tf_op jit(solution)/shard_map/reduce_scatter | solution.py:67
  544.5 0.7 broadcast_maximum_fusion
  545.2 449.9 %reduce-scatter.3.cloned.1.call-done = f32[8,10,128]{2,0,1:T(8,128)} async-done(((f32[8,10,8192]{2,0,1:T(8,128)}), f32[8,10,128]{2,0,1:T(8,128)}) %reduce-scatter.3.cloned.1.call-update) | async-done | bytes 40976 | tf_op jit(solution)/shard_map/reduce_scatter | solution.py:66
  995.1 0.8 divide_convert_fusion
  995.9 0.0 copy-start.2
  995.9 0.1 reshape.105
  996.0 0.6 copy.99
  996.6 0.0 all-gather.2.cloned.1.call-update
  996.6 125.3 %all-gather.2.cloned.1.call-done = bf16[8,10,128,64]{3,0,1,2:T(8,128)(2,1)} async-done(((bf16[8,10,2,64]{3,0,1,2:T(8,128)(2,1)}), bf16[8,10,128,64]{3,0,1,2:T(8,128)(2,1)}) %all-gather.2.cloned.1.call-update) | async-done | bytes 1310736 | tf_op jit(solution)/shard_map/all_gather | solution.py:72
  1121.9 4.4 copy.100
  1126.3 25.0 %copy.101 = f32[8,10,128,64]{1,0,3,2:T(8,128)} copy(bf16[8,10,128,64]{2,3,1,0:T(8,128)(2,1)S(1)} %copy.100) | data formatting | bytes 3932160 | tf_op jit(solution)/shard_map/reshape | solution.py:14
  1151.3 0.0 copy-done.2
  1151.3 16.3 %reduce_sum.68 = f32[8,10,64,32]{1,0,3,2:T(8,128)} reduce(f32[8,10,64,2,32,2]{1,0,5,4,3,2:T(8,128)} %bitcast.56, f32[]{:T(128)} %constant.53.clone.1), dimensions={3,5}, to_apply=%region_4.5 | reduce | flops 491520 | bytes 3276804 | tf_op jit(solution)/shard_map/reduce_sum | solution.py:15
  1167.6 6.4 multiply_convert_fusion
  1174.0 7.0 copy.102
  1181.0 3.4 convert_reduce_fusion
  1184.4 0.0 copy-start.1
  1184.4 0.2 multiply_convert_fusion.1
  1184.6 2.3 copy.103
  1186.9 0.2 convert_reduce_fusion.1
  1187.1 0.1 multiply_convert_fusion.2
  1187.2 1.2 copy.104
  1188.4 0.1 convert_reduce_fusion.2
  1188.5 0.7 copy.105
  1189.2 0.6 copy.106
  1189.8 0.0 copy-done.1
  (7 shorter events, 0.1 us)
Async XLA Ops:
  7.2 21.7 %copy-start = (bf16[1,8,10,8192]{3,1,2,0:T(8,128)(2,1)S(1)}, bf16[1,8,10,8192]{3,1,2,0:T(8,128)(2,1)}, u32[]{:S(2)}) copy-start(bf16[1,8,10,8192]{3,1,2,0:T(8,128)(2,1)} %param.3) | copy-start | bytes 3932164
  10.5 33.5 %all-to-all-start = ((bf16[8,2,1,8192]{3,1,2,0:T(2,128)(2,1)}), bf16[8,2,1,8192]{3,1,2,0:T(2,128)(2,1)S(1)}, u32[]{:S(2)}, u32[]{:S(2)}) async-start(bf16[8,2,1,8192]{3,1,2,0:T(2,128)(2,1)} %bitcast.6), calls=%async_computation | async-start | bytes 524288 | tf_op jit(solution)/shard_map/all_to_all | solution.py:57
  44.0 14.0 %copy-start.3 = (s32[512,8]{0,1:T(8,128)S(1)}, s32[512,8]{0,1:T(8,128)}, u32[]{:S(2)}) copy-start(s32[512,8]{0,1:T(8,128)} %param.5) | copy-start | bytes 49156
  44.1 63.9 %all-to-all-start.1 = ((bf16[8,2,10,8192]{3,1,2,0:T(2,128)(2,1)}), bf16[8,2,10,8192]{3,1,2,0:T(2,128)(2,1)}, u32[]{:S(2)}, u32[]{:S(2)}) async-start(bf16[8,2,10,8192]{3,1,2,0:T(2,128)(2,1)} %copy.94), calls=%async_computation.1 | async-start | bytes 5242880 | tf_op jit(solution)/shard_map/all_to_all | solution.py:56
  58.0 486.6 %reduce-scatter.5.cloned.1.call-start = ((), (), s32[]{:S(2)}) async-start(), calls=%async_computation.5 | async-start | bytes 266240 | tf_op jit(solution)/shard_map/reduce_scatter | solution.py:67
  60.1 935.0 %reduce-scatter.3.cloned.1.call-start = ((), (), s32[]{:S(2)}) async-start(), calls=%async_computation.4 | async-start | bytes 2662400 | tf_op jit(solution)/shard_map/reduce_scatter | solution.py:66
  115.3 1006.6 %all-gather.2.cloned.1.call-start = ((), (), s32[]{:S(2)}) async-start(), calls=%async_computation.6 | async-start | bytes 2662400 | tf_op jit(solution)/shard_map/all_gather | solution.py:72
  995.9 155.4 %copy-start.2 = (bf16[8,10,128]{2,0,1:T(8,128)(2,1)}, bf16[8,10,128]{2,0,1:T(8,128)(2,1)S(1)}, u32[]{:S(2)}) copy-start(bf16[8,10,128]{2,0,1:T(8,128)(2,1)S(1)} %divide_convert_fusion) | copy-start | bytes 61444
  1184.4 5.4 copy-start.1
Sparse Core Ops, SparseCore 0:
  62.2 482.3 reduce-scatter.4
  547.5 447.5 reduce-scatter.2
  997.8 124.0 all-gather.1
where the time goes:
time: 1200 us
  waiting for transfers between devices  1050 us (88%)
  local copies, waits for them, and re-layouts  56.9 us (5%)
  starting transfers between devices  32.4 us (3%)
  other arithmetic  28.9 us (2%)
  between operations  13.9 us (1%)
  matrix products  12.2 us (1%)
    reduce_scatter x1, waiting for transfers between devices, on_device(): lax.psum_scatter(local_sums, 'scene', scatter_dimension=2, tiled=True)  450 us
    reduce_scatter x1, waiting for transfers between devices, on_device(): lax.psum_scatter(local_totals, 'scene', scatter_dimension=1, tiled=True)  429 us
    all_gather x1, waiting for transfers between devices, on_device(): whole_grid = lax.all_gather(grid, 'scene', axis=2, tiled=True)  125 us
    all_to_all x1, waiting for transfers between devices, on_device(): lax.all_to_all(send_rad, 'tile', split_axis=0, concat_axis=0, tiled=True)  47.7 us
    reshape x1, local copies, waits for them, and re-layouts, average_pool(): values.astype(jnp.float32)  25 us
  transfers between devices with their start and end apart: 5, of which 5 were waited for; matrix products, arithmetic and copies ran while one was open for 2% of the time, Pallas kernels for 0%

commit v1 on v0

v1 whole, which is shorter than its diff:
```python
import functools

import jax
import jax.numpy as jnp
from jax import lax
from jax.experimental import pallas as pl
from jax.experimental.pallas import tpu as pltpu
from jax.sharding import PartitionSpec as P

MESH = pl.DeviceIdType.MESH
K = 8
BANDS = 10
TILES = 64
PIX = 8192
LANES = 128
MSG = 96
BOX = 64
F32 = jnp.float32
BF16 = jnp.bfloat16


def offsets(i):
    dx = lax.rem(i, 4)
    dy = lax.rem(lax.div(i, 4) + i, 4)
    dc = lax.rem(lax.div(i, 16), 2)
    dz = lax.div(i, 32)
    return dx, dy, dc, dz


def position():
    scene = lax.axis_index("scene")
    tile = lax.axis_index("tile")
    z_lo = lax.div(scene, 8)
    x = lax.rem(lax.div(scene, 2), 4)
    core = lax.rem(scene, 2)
    z_hi = lax.div(tile, 4)
    y = lax.rem(tile, 4)
    return z_lo, x, core, z_hi, y


def exchange_kernel(
    rad_ref, weight_ref, foot_ref, rows_ref, comp_ref,
    rad, weight, foot, turn, send, recv, assign, acc, send3, recv3, line,
    in_sem, send_sem, recv_sem, send3_sem, recv3_sem, sg1_sem, rg1_sem, sg2_sem, rg2_sem,
):
    z_lo, x, core, z_hi, y = position()
    tile = z_hi * 4 + y
    xc = x * 2 + core
    pair = lax.div(z_lo, 2)
    odd = lax.rem(z_lo, 2)

    load_foot = pltpu.make_async_copy(foot_ref.at[pl.ds(pl.multiple_of(pair * 128, 128), 128)], foot, in_sem.at[2])
    load_weight = pltpu.make_async_copy(weight_ref.at[0], weight, in_sem.at[1])
    load_rad = pltpu.make_async_copy(rad_ref.at[0], rad, in_sem.at[0])
    load_weight.start()
    load_rad.start()
    load_foot.start()

    def box_device(i):
        dx, dy, dc, dz = offsets(i)
        x2 = lax.rem(x + dx, 4)
        y2 = lax.rem(y + dy, 4)
        c2 = lax.rem(core + dc, 2)
        o2 = lax.rem(odd + dz, 2)
        block = (2 * y2 + o2) * 8 + x2 * 2 + c2
        return block, ((2 * pair + o2) * 8 + x2 * 2 + c2, z_hi * 4 + y2)

    def owner_device(o):
        return ((2 * y + odd) * 8 + xc, o)

    def source_device(s):
        return ((2 * lax.rem(s, 4) + odd) * 8 + xc, lax.div(s, 4) * 4 + pair)

    my_source = z_hi * 4 + pair
    at_home = pair == y

    barrier = pltpu.get_barrier_semaphore()

    def greet_box(i, _):
        _, device = box_device(i)
        pl.semaphore_signal(barrier, inc=1, device_id=device, device_id_type=MESH)
        return 0

    lax.fori_loop(1, BOX, greet_box, 0)

    def greet_source(s, _):
        @pl.when(jnp.logical_not(jnp.logical_and(at_home, s == my_source)))
        def _():
            pl.semaphore_signal(barrier, inc=1, device_id=source_device(s), device_id_type=MESH)
        return 0

    lax.fori_loop(0, 8, greet_source, 0)

    def line_device(i):
        z2 = lax.rem(z_lo + i, 8)
        return z2, (z2 * 8 + xc, tile)

    def greet_line(i, _):
        pl.semaphore_signal(barrier, inc=1, device_id=line_device(i)[1], device_id_type=MESH)
        return 0

    lax.fori_loop(1, 8, greet_line, 0)

    load_foot.wait()
    lane = lax.broadcasted_iota(jnp.int32, (128, 16 * BOX), 1)
    row = lax.broadcasted_iota(jnp.int32, (128, 16 * BOX), 0)
    slot = lax.div(lane, 16)
    dx, dy, dc, dz = offsets(slot)
    source_row = (
        lax.rem(odd + dz, 2) * 64
        + lax.rem(x + 4 - dx, 4) * 16
        + lax.rem(core + dc, 2) * 8
        + z_hi * 4
        + lax.rem(y + 4 - dy, 4)
    )
    pick = jnp.where(row == source_row, 1.0, 0.0).astype(BF16)
    named = lax.dot_general(
        foot[...].astype(F32).astype(BF16), pick, (((0,), (0,)), ((), ())), preferred_element_type=F32
    )
    own = lax.broadcasted_iota(jnp.int32, (K, 16 * BOX), 0) == lax.rem(
        lax.broadcasted_iota(jnp.int32, (K, 16 * BOX), 1), 8
    )
    target = jnp.sum(jnp.where(own, named, 0.0), axis=0, keepdims=True)
    half = lax.rem(lax.div(lane, 8), 2)
    wanted = jnp.where(lax.div(row, 64) == half, lax.rem(row, 64).astype(F32), -1.0)
    assign[...] = jnp.where(wanted == target, 1.0, 0.0).astype(BF16)

    load_weight.wait()
    load_rad.wait()
    pl.semaphore_wait(barrier, BOX - 1 + 7 + 8 - jnp.where(at_home, 1, 0))

    def fill(block, out):
        pixels = pl.ds(pl.multiple_of(block * LANES, LANES), LANES)
        for k in range(K):
            turn[16 * k : 16 * k + BANDS, :] = rad[k, :, pixels].astype(F32)
        w = weight[:, pixels].astype(F32)
        for j in range(5):
            low = turn[pl.ds(2 * j, K, stride=16), :] * w
            high = turn[pl.ds(2 * j + 1, K, stride=16), :] * w
            out[16 * j : 16 * j + 16, :] = jnp.concatenate([low, high], axis=0).astype(BF16)
        out[80:96, :] = jnp.concatenate([w, jnp.zeros_like(w)], axis=0).astype(BF16)

    def box_copy(i):
        block, device = box_device(i)
        copy = pltpu.make_async_remote_copy(
            src_ref=send.at[i], dst_ref=recv.at[i], send_sem=send_sem.at[i], recv_sem=recv_sem.at[i],
            device_id=device, device_id_type=MESH,
        )
        return block, copy

    def send_box(i, _):
        block, copy = box_copy(i)
        fill(block, send.at[i])
        copy.start()
        return 0

    lax.fori_loop(1, BOX, send_box, 0)
    fill((2 * y + odd) * 8 + xc, recv.at[0])

    def wait_box(i, _):
        box_copy(i)[1].wait_recv()
        return 0

    for g in range(4):
        lax.fori_loop(max(16 * g, 1), 16 * g + 16, wait_box, 0)
        left = assign[:, 256 * g : 256 * g + 256]
        for j in range(0, 6, 2):
            right = jnp.concatenate(
                [recv[16 * g : 16 * g + 16, 16 * h : 16 * h + 16, :].reshape(256, LANES) for h in (j, j + 1)], axis=1
            )
            part = jnp.dot(left, right, preferred_element_type=F32)
            if g == 0:
                acc[:, LANES * j : LANES * j + 2 * LANES] = part
            else:
                acc[:, LANES * j : LANES * j + 2 * LANES] += part

    for o in range(8):
        for j in range(6):
            lanes = slice(LANES * j, LANES * j + LANES)
            both = jnp.concatenate([acc[8 * o : 8 * o + 8, lanes], acc[64 + 8 * o : 72 + 8 * o, lanes]], axis=0)
            send3[o, 16 * j : 16 * j + 16, :] = both.astype(BF16)

    def owner_copy(o):
        return pltpu.make_async_remote_copy(
            src_ref=send3.at[o], dst_ref=recv3.at[my_source], send_sem=send3_sem.at[o], recv_sem=recv3_sem.at[my_source],
            device_id=owner_device(o), device_id_type=MESH,
        )

    def stays(o):
        return jnp.logical_and(at_home, o == tile)

    def send_owner(i, _):
        o = lax.rem(tile + i, 8)

        @pl.when(jnp.logical_not(stays(o)))
        def _():
            owner_copy(o).start()
        return 0

    lax.fori_loop(0, 8, send_owner, 0)

    @pl.when(at_home)
    def _():
        recv3[my_source] = send3[tile]

    def wait_source(s, _):
        @pl.when(jnp.logical_not(jnp.logical_and(at_home, s == my_source)))
        def _():
            pltpu.make_async_remote_copy(
                src_ref=send3.at[s], dst_ref=recv3.at[s], send_sem=send3_sem.at[s], recv_sem=recv3_sem.at[s],
                device_id=source_device(s), device_id_type=MESH,
            ).wait_recv()
        return 0

    lax.fori_loop(0, 8, wait_source, 0)

    total = recv3[0].astype(F32)
    for s in range(1, 8):
        total = total + recv3[s].astype(F32)
    scale = jnp.maximum(total[80:88, :], 1.0)
    mean = [(total[8 * b : 8 * b + 8, :] / scale).astype(BF16).astype(F32) for b in range(BANDS)]
    comp_ref[...] = jnp.concatenate(mean, axis=0)

    blank = jnp.zeros((8, LANES), F32)
    mean = mean + [blank] * 3
    pixel = lax.broadcasted_iota(jnp.int32, (LANES, LANES), 0)
    spot = lax.broadcasted_iota(jnp.int32, (LANES, LANES), 1)
    pooled = None
    for g in range(4):
        left = jnp.concatenate([mean[3 * g + b] if b < 3 else blank for b in range(4)], axis=0).astype(BF16)
        mix = jnp.where(spot == 32 * g + lax.div(lax.rem(pixel, 64), 2), 0.25, 0.0).astype(BF16)
        part = jnp.dot(left, mix, preferred_element_type=F32)
        pooled = part if pooled is None else pooled + part
    line[z_lo] = pooled.astype(BF16)

    def line_copy(i):
        return pltpu.make_async_remote_copy(
            src_ref=line.at[z_lo], dst_ref=line.at[z_lo], send_sem=sg1_sem.at[i], recv_sem=rg1_sem.at[z_lo],
            device_id=line_device(i)[1], device_id_type=MESH,
        )

    def send_line(i, _):
        line_copy(i).start()
        return 0

    lax.fori_loop(1, 8, send_line, 0)

    def wait_line(i, _):
        z2, device = line_device(i)
        pltpu.make_async_remote_copy(
            src_ref=line.at[z2], dst_ref=line.at[z2], send_sem=sg1_sem.at[i], recv_sem=rg1_sem.at[z2],
            device_id=device, device_id_type=MESH,
        ).wait_recv()
        return 0

    lax.fori_loop(1, 8, wait_line, 0)

    def plane_device(i):
        xc2 = lax.rem(xc + i, 8)
        return xc2, (z_lo * 8 + xc2, tile)

    def plane_copy(i):
        return pltpu.make_async_remote_copy(
            src_ref=line, dst_ref=rows_ref.at[xc], send_sem=sg2_sem.at[i], recv_sem=rg2_sem.at[xc],
            device_id=plane_device(i)[1], device_id_type=MESH,
        )

    def send_plane(i, _):
        plane_copy(i).start()
        return 0

    lax.fori_loop(1, 8, send_plane, 0)
    rows_ref[xc] = line[...]

    def wait_plane(i, _):
        xc2, device = plane_device(i)
        pltpu.make_async_remote_copy(
            src_ref=line, dst_ref=rows_ref.at[xc2], send_sem=sg2_sem.at[i], recv_sem=rg2_sem.at[xc2],
            device_id=device, device_id_type=MESH,
        ).wait_recv()
        return 0

    lax.fori_loop(1, 8, wait_plane, 0)

    def drain_box(i, _):
        box_copy(i)[1].wait_send()
        return 0

    lax.fori_loop(1, BOX, drain_box, 0)

    def drain_owner(o, _):
        @pl.when(jnp.logical_not(stays(o)))
        def _():
            owner_copy(o).wait_send()
        return 0

    lax.fori_loop(0, 8, drain_owner, 0)

    def drain_rows(i, _):
        line_copy(i).wait_send()
        plane_copy(i).wait_send()
        return 0

    lax.fori_loop(1, 8, drain_rows, 0)


def exchange(radiance, cloud_weight, footprint):
    any_space = pl.BlockSpec(memory_space=pl.ANY)
    vmem = pl.BlockSpec(memory_space=pltpu.VMEM)
    dma = pltpu.SemaphoreType.DMA
    return pl.pallas_call(
        exchange_kernel,
        out_shape=(
            jax.ShapeDtypeStruct((8, 8, 32, LANES), BF16),
            jax.ShapeDtypeStruct((80, LANES), F32),
        ),
        in_specs=[any_space] * 3,
        out_specs=(vmem, vmem),
        scratch_shapes=[
            pltpu.VMEM((K, BANDS, PIX), BF16),
            pltpu.VMEM((K, PIX), jnp.int32),
            pltpu.VMEM((128, K), jnp.int32),
            pltpu.VMEM((128, LANES), F32),
            pltpu.VMEM((BOX, MSG, LANES), BF16),
            pltpu.VMEM((BOX, MSG, LANES), BF16),
            pltpu.VMEM((128, 16 * BOX), BF16),
            pltpu.VMEM((128, 6 * LANES), F32),
            pltpu.VMEM((8, MSG, LANES), BF16),
            pltpu.VMEM((8, MSG, LANES), BF16),
            pltpu.VMEM((8, 32, LANES), BF16),
            dma((3,)),
            dma((BOX,)),
            dma((BOX,)),
            dma((8,)),
            dma((8,)),
            dma((8,)),
            dma((8,)),
            dma((8,)),
            dma((8,)),
        ],
        compiler_params=pltpu.CompilerParams(
            collective_id=0, has_side_effects=True, vmem_limit_bytes=40 * 1024 * 1024
        ),
        name="exchange",
    )(radiance, cloud_weight, footprint)


def pyramid_kernel(rows_ref, comp_ref, composite, one, two, three, four, five, t1, t2, t3, t4, t5):
    for t in range(8):
        composite[t] = comp_ref[pl.ds(t, BANDS, stride=8), :].astype(BF16)

    before = lax.broadcasted_iota(jnp.int32, (LANES, LANES), 0)
    after = lax.broadcasted_iota(jnp.int32, (LANES, LANES), 1)
    same = lax.div(before, 32) == lax.div(after, 32)
    mix = jnp.where(
        jnp.logical_and(same, lax.div(lax.rem(before, 32), 2) == lax.rem(after, 32)), 0.25, 0.0
    ).astype(BF16)

    def halve(values):
        n = values.shape[0]
        flat = values.reshape(-1, LANES)
        wide = jnp.dot(flat, mix, preferred_element_type=F32).reshape(n, -1, LANES)
        return wide

    def keep(scratch, row, values):
        for i in range(8):
            at = row(i) * 24
            scratch[at : at + 24, :] = values[i, 0:24, :].astype(F32)

    level = [rows_ref[xc] for xc in range(8)]
    for xc in range(8):
        keep(t1, lambda i, xc=xc: i * 8 + xc, level[xc])
    for scratch, m in ((t2, 4), (t3, 2), (t4, 1)):
        level = [(halve(level[2 * q]) + halve(level[2 * q + 1])).astype(BF16) for q in range(m)]
        for q in range(m):
            keep(scratch, lambda i, q=q, m=m: i * m + q, level[q])
    last = halve(level[0])
    for i in range(4):
        both = (last[2 * i] + last[2 * i + 1]).astype(BF16)
        t5[24 * i : 24 * i + 24, :] = both[0:24, :].astype(F32)

    for scratch, out, height, width in (
        (t1, one, 64, 32), (t2, two, 32, 16), (t3, three, 16, 8), (t4, four, 8, 4), (t5, five, 4, 2)
    ):
        for r in range(24):
            lines = scratch[pl.ds(r, height, stride=24), :].astype(BF16)
            for g in range(4):
                b = 3 * g + r // 8
                if b < BANDS:
                    out[r % 8, b] = lines[:, 32 * g : 32 * g + width]


def pyramid(rows, comp):
    vmem = pl.BlockSpec(memory_space=pltpu.VMEM)
    shapes = [(8, BANDS, LANES)] + [(8, BANDS, 64 >> i, 32 >> i) for i in range(5)]
    return pl.pallas_call(
        pyramid_kernel,
        out_shape=[jax.ShapeDtypeStruct(s, BF16) for s in shapes],
        in_specs=[vmem] * 2,
        out_specs=[vmem] * 6,
        scratch_shapes=[pltpu.VMEM((24 * (64 >> i), LANES), F32) for i in range(5)],
        compiler_params=pltpu.CompilerParams(vmem_limit_bytes=40 * 1024 * 1024),
        name="pyramid",
    )(rows, comp)


def on_device(radiance, cloud_weight, footprint):
    rows, comp = exchange(radiance, cloud_weight, footprint)
    return tuple(pyramid(rows, comp))


def solution(mesh):
    in_specs = (P(("scene", "tile"), None, None, None), P(("scene", "tile"), None, None), P())
    out_specs = (
        P("tile", None, "scene"),
        P("tile", None, None, None),
        P("tile", None, None, None),
        P("tile", None, None, None),
        P("tile", None, None, None),
        P("tile", None, None, None),
    )
    return jax.shard_map(
        on_device, mesh=mesh, in_specs=in_specs, out_specs=out_specs, check_vma=False
    )
```

time: 1200 us -> 85.9 us (0.07)
  waiting for transfers between devices: 1050 us -> 0 us
  Pallas kernels: 0 us -> 76.3 us
  local copies, waits for them, and re-layouts: 56.9 us -> 8.71 us
  starting transfers between devices: 32.4 us -> 0 us
  other arithmetic: 28.9 us -> 0 us
  between operations: 13.9 us -> 0.67 us
  matrix products: 12.2 us -> 0 us
    reduce_scatter x2 -> x0, waiting for transfers between devices: 879 us -> none  [the longest x1 450 us: on_device(): lax.psum_scatter(local_sums, 'scene', scatter_dimension=2, tiled=True)]
    all_gather x1 -> x0, waiting for transfers between devices: 125 us -> none  [on_device(): whole_grid = lax.all_gather(grid, 'scene', axis=2, tiled=True)]
    pallas_call x0 -> x2, Pallas kernels: none -> 76.3 us  [the longest x1 75.1 us: exchange(): pl.pallas_call(exchange_kernel, out_shape=(jax.ShapeDtypeStruct((8, 8, 32...]
    all_to_all x2 -> x0, waiting for transfers between devices: 47.8 us -> none  [the longest x1 47.7 us: on_device(): lax.all_to_all(send_rad, 'tile', split_axis=0, concat_axis=0, tiled=True)]
    reshape x6 -> x0, local copies, waits for them, and re-layouts: 39.4 us -> none  [the longest x1 25 us: average_pool(): values.astype(jnp.float32)]
    all_to_all x2 -> x0, starting transfers between devices: 32.1 us -> none  [the longest x1 18.3 us: on_device(): lax.all_to_all(send_weight, 'tile', split_axis=0, concat_axis=0, tiled=True)]
    reduce_sum x7 -> x0, other arithmetic: 20.4 us -> none  [the longest x5 20 us: average_pool(): return jnp.mean(shaped, axis=(-3, -1)).astype(jnp.bfloat16)]
    dot_general x5 -> x0, matrix products: 12.2 us -> none  [the longest x1 7.29 us: on_device(): jnp.einsum('scu,scbq->ubq', assign, product, precision=lax.Precision.HIGH...]
  transfers between devices with their start and end apart: 5 -> 0, of which waited for: 5 -> 0; matrix products, arithmetic and copies ran while one was open for 2% -> 0% of each run, Pallas kernels for 0% -> 0%
where the time goes in v1:
time: 85.9 us; the launch traced here: 85.7 us
  Pallas kernels  76.3 us (89%)
  local copies, waits for them, and re-layouts  8.71 us (10%)
    pallas_call x1, Pallas kernels, exchange(): pl.pallas_call(exchange_kernel, out_shape=(jax.ShapeDtypeStruct((8, 8, 32...  75.1 us
    pallas_call x6, local copies, waits for them, and re-layouts, pyramid(): pl.pallas_call(pyramid_kernel, out_shape=[jax.ShapeDtypeStruct(s, BF16) f...  5.75 us
    unnamed x4, local copies, waits for them, and re-layouts  2.96 us

profile of v1, /device:TPU:1, one launch (start us, length us, event | category | flops | bytes accessed | tf_op | source)
XLA Modules:
  0.0 85.7 jit_solution(12710675814480548663)
XLA Ops:
  0.6 0.8 copy.10.foot_ref
  1.5 0.0 copy-start
  1.5 2.1 %copy.9.rad_ref = bf16[1,8,10,8192]{3,2,1,0:T(8,128)(2,1)S(1)} copy(bf16[1,8,10,8192]{3,1,2,0:T(8,128)(2,1)} %param.3) | data formatting | bytes 2621440 | tf_op args[0]
  3.6 0.0 copy-done
  3.6 75.1 %exchange.1 = (bf16[8,8,32,128]{3,2,1,0:T(8,128)(2,1)S(1)}, f32[80,128]{1,0:T(8,128)S(1)}) custom-call(bf16[1,8,10,8192]{3,2,1,0:T(8,128)(2,1)S(1)} %copy.9.rad_ref, s32[1,8,8192]{2,1,0:T(8,128)S(1)} %copy-done, s32[512,8]{1,0:T(8,128)S(1)} %copy.10.foot_ref), custom_call_target="tpu_custom_call" | custom-call | tf_op jit(solution)/shard_map/exchange/pallas_call | solution.py:311
  78.7 1.2 %pyramid.1 = (bf16[8,10,128]{2,1,0:T(8,128)(2,1)S(1)}, bf16[8,10,64,32]{3,2,1,0:T(8,128)(2,1)S(1)}, bf16[8,10,32,16]{3,2,1,0:T(8,128)(2,1)S(1)}, bf16[8,10,16,8]...) custom-call(bf16[8,8,32,128]{3,2,1,0:T(8,128)(2,1)S(1)} %get-tuple-element.8.rows_ref, ...), custom_call_target="tpu_custom_call" | custom-call | tf_op jit(solution)/shard_map/pyramid/pallas_call | solution.py:396
  79.9 0.6 copy.11
  80.5 0.9 %copy.16 = bf16[8,10,4,2]{1,3,2,0:T(2,128)(2,1)} copy(bf16[8,10,4,2]{3,2,1,0:T(4,128)(2,1)S(1)} %get-tuple-element.15) | data formatting | bytes 2560 | tf_op jit(solution)/shard_map/pyramid/pallas_call | solution.py:396
  81.4 1.1 %copy.15 = bf16[8,10,8,4]{1,3,2,0:T(4,128)(2,1)} copy(bf16[8,10,8,4]{3,2,1,0:T(8,128)(2,1)S(1)} %get-tuple-element.14) | data formatting | bytes 10240 | tf_op jit(solution)/shard_map/pyramid/pallas_call | solution.py:396
  82.6 0.8 copy.14
  83.4 1.0 %copy.13 = bf16[8,10,32,16]{2,3,1,0:T(8,128)(2,1)} copy(bf16[8,10,32,16]{3,2,1,0:T(8,128)(2,1)S(1)} %get-tuple-element.12) | data formatting | bytes 163840 | tf_op jit(solution)/shard_map/pyramid/pallas_call | solution.py:396
  84.3 1.3 %copy.12 = bf16[8,10,64,32]{2,3,1,0:T(8,128)(2,1)} copy(bf16[8,10,64,32]{3,2,1,0:T(8,128)(2,1)S(1)} %get-tuple-element.11) | data formatting | bytes 655360 | tf_op jit(solution)/shard_map/pyramid/pallas_call | solution.py:396
Async XLA Ops:
  1.5 2.1 %copy-start = (s32[1,8,8192]{2,1,0:T(8,128)S(1)}, s32[1,8,8192]{2,1,0:T(8,128)}, u32[]{:S(2)}) copy-start(s32[1,8,8192]{2,1,0:T(8,128)} %weight_ref.1) | copy-start | bytes 786436

commit v2 on v0

v2 whole, which is shorter than its diff:
```python
import functools

import jax
import jax.numpy as jnp
from jax import lax
from jax.experimental import pallas as pl
from jax.experimental.pallas import tpu as pltpu
from jax.sharding import PartitionSpec as P

MESH = pl.DeviceIdType.MESH
K = 8
BANDS = 10
TILES = 64
PIX = 8192
LANES = 128
HALF = 48
BOX = 64
F32 = jnp.float32
BF16 = jnp.bfloat16


STEPS = (
    (2, 2), (2, 1), (1, 2), (2, 3), (3, 2), (2, 0), (1, 1), (0, 2), (3, 3), (1, 3), (3, 1), (1, 0), (0, 1), (3, 0), (0, 3),
)
STEPS_X = sum(step[0] * 4**n for n, step in enumerate(STEPS))
STEPS_Y = sum(step[1] * 4**n for n, step in enumerate(STEPS))


def each_partner(visit):
    def inner(u, carry):
        n, dx, dy = carry
        visit(4 * n + u, dx, dy, 1 - lax.rem(u, 2), 1 - lax.div(u, 2))
        return carry

    def outer(n, carry):
        in_x, in_y = carry
        lax.fori_loop(0, 4, inner, (n, lax.rem(in_x, 4), lax.rem(in_y, 4)))
        return lax.div(in_x, 4), lax.div(in_y, 4)

    lax.fori_loop(0, 15, outer, (jnp.int32(STEPS_X), jnp.int32(STEPS_Y)))
    lax.fori_loop(0, 3, inner, (jnp.int32(15), jnp.int32(0), jnp.int32(0)))


def position():
    scene = lax.axis_index("scene")
    tile = lax.axis_index("tile")
    z_lo = lax.div(scene, 8)
    x = lax.rem(lax.div(scene, 2), 4)
    core = lax.rem(scene, 2)
    z_hi = lax.div(tile, 4)
    y = lax.rem(tile, 4)
    return z_lo, x, core, z_hi, y


def exchange_kernel(
    rad_ref, weight_ref, foot_ref, rows_ref, comp_ref,
    rad, weight, foot, send, recv, assign, acc, send3, recv3, line,
    ring_sem, in_sem, send_sem, recv_sem, send3_sem, recv3_sem, sg1_sem, rg1_sem, sg2_sem, rg2_sem,
):
    z_lo, x, core, z_hi, y = position()
    tile = z_hi * 4 + y
    xc = x * 2 + core
    pair = lax.div(z_lo, 2)
    odd = lax.rem(z_lo, 2)

    load_foot = pltpu.make_async_copy(foot_ref.at[:, pl.ds(pl.multiple_of(pair * 128, 128), 128)], foot, in_sem.at[2])
    load_weight = pltpu.make_async_copy(weight_ref.at[0], weight, in_sem.at[1])
    load_rad = pltpu.make_async_copy(rad_ref.at[0], rad, in_sem.at[0])
    load_weight.start()
    load_rad.start()
    load_foot.start()

    def box_device(dx, dy, dc, dz):
        x2 = lax.rem(x + dx, 4)
        y2 = lax.rem(y + dy, 4)
        c2 = lax.rem(core + dc, 2)
        o2 = lax.rem(odd + dz, 2)
        block = (2 * y2 + o2) * 8 + x2 * 2 + c2
        return block, ((2 * pair + o2) * 8 + x2 * 2 + c2, z_hi * 4 + y2)

    ring = z_hi * 4 + pair

    def ring_device(step):
        box = lax.rem(ring + step, 8)
        return ((2 * lax.rem(box, 4) + odd) * 8 + xc, lax.div(box, 4) * 4 + y)

    def owner_device(o):
        return ((2 * y + odd) * 8 + xc, o)

    def source_device(s):
        return ((2 * lax.rem(s, 4) + odd) * 8 + xc, lax.div(s, 4) * 4 + pair)

    my_source = z_hi * 4 + pair
    at_home = pair == y

    barrier = pltpu.get_barrier_semaphore()

    def greet(slot, *offset):
        pl.semaphore_signal(barrier, inc=1, device_id=box_device(*offset)[1], device_id_type=MESH)

    each_partner(greet)
    for step in (1, 7):
        pl.semaphore_signal(barrier, inc=1, device_id=ring_device(step), device_id_type=MESH)

    def tell_ring():
        pl.semaphore_signal(ring_sem.at[0], inc=1, device_id=ring_device(1), device_id_type=MESH)
        pl.semaphore_signal(ring_sem.at[1], inc=1, device_id=ring_device(7), device_id_type=MESH)

    def hear_ring():
        pl.semaphore_wait(ring_sem.at[0], 1)
        pl.semaphore_wait(ring_sem.at[1], 1)

    def line_device(i):
        z2 = lax.rem(z_lo + i, 8)
        return z2, (z2 * 8 + xc, tile)

    load_weight.wait()
    load_rad.wait()
    pl.semaphore_wait(barrier, BOX - 1 + 2)
    tell_ring()

    def fill(h, block, out):
        pixels = pl.ds(pl.multiple_of(block * LANES, LANES), LANES)
        w = weight[:, pixels].astype(F32)
        twice = jnp.concatenate([w, w], axis=0).astype(BF16)
        if h == 0:
            first = jnp.concatenate([w, w * rad[0, :, pixels].astype(F32)], axis=0).astype(BF16)
            out[0:16, :] = first
            for j in range(2):
                out[16 * j + 16 : 16 * j + 32, :] = rad[2 * j + 1 : 2 * j + 3, :, pixels].reshape(16, LANES) * twice
        else:
            for j in range(2):
                out[16 * j : 16 * j + 16, :] = rad[2 * j + 5 : 2 * j + 7, :, pixels].reshape(16, LANES) * twice
            last = jnp.concatenate([w * rad[9, :, pixels].astype(F32), jnp.zeros_like(w)], axis=0).astype(BF16)
            out[32:48, :] = last

    def box_copy(h, slot, device):
        return pltpu.make_async_remote_copy(
            src_ref=send.at[h, slot], dst_ref=recv.at[h, slot],
            send_sem=send_sem.at[h, slot], recv_sem=recv_sem.at[h, slot],
            device_id=device, device_id_type=MESH,
        )

    other_core = box_device(0, 0, 1, 0)[1]

    for h in range(2):
        def send_box(slot, *offset, h=h):
            block, device = box_device(*offset)
            fill(h, block, send.at[h, slot])
            box_copy(h, slot, device).start()

        each_partner(send_box)
        fill(h, (2 * y + odd) * 8 + xc, recv.at[h, BOX - 1])
        hear_ring()
        tell_ring()

    load_foot.wait()
    lane = lax.broadcasted_iota(jnp.int32, (1, 16 * BOX), 1)
    slot = lane >> 4
    step = slot >> 2
    dx, dy = jnp.zeros_like(slot), jnp.zeros_like(slot)
    for n, (far_x, far_y) in enumerate(STEPS):
        dx = jnp.where(step == n, far_x, dx)
        dy = jnp.where(step == n, far_y, dy)
    source_row = (
        (((odd + 1 - ((slot >> 1) & 1)) & 1) << 6)
        + (((x - dx) & 3) << 4)
        + (((core + 1 - (slot & 1)) & 1) << 3)
        + ((y - dy) & 3)
        + z_hi * 4
    )
    pick = jnp.where(lax.broadcasted_iota(jnp.int32, (128, 16 * BOX), 0) == source_row, 1.0, 0.0).astype(BF16)
    named = jnp.dot(foot[...].astype(F32).astype(BF16), pick, preferred_element_type=F32)
    own = lax.broadcasted_iota(jnp.int32, (K, 16 * BOX), 0) == (lane & 7)
    target = jnp.sum(jnp.where(own, named, 0.0), axis=0, keepdims=True).astype(jnp.int32) + ((lane & 8) << 3)
    row = lax.broadcasted_iota(jnp.int32, (128, 16 * BOX), 0)
    assign[...] = jnp.where(row == target, 1.0, 0.0).astype(BF16)
    hear_ring()
    tell_ring()

    def stays(o):
        return jnp.logical_and(at_home, o == tile)

    def owner_copy(h, o):
        return pltpu.make_async_remote_copy(
            src_ref=send3.at[h, o], dst_ref=recv3.at[h, my_source],
            send_sem=send3_sem.at[h, o], recv_sem=recv3_sem.at[h, my_source],
            device_id=owner_device(o), device_id_type=MESH,
        )

    def reduce_box(h):
        def wait_box(i, _):
            box_copy(h, i, other_core).wait_recv()
            return 0

        for g in range(4):
            lax.fori_loop(16 * g, min(16 * g + 16, BOX - 1), wait_box, 0)
            left = assign[:, 256 * g : 256 * g + 256]
            right = jnp.concatenate(
                [recv[h, 16 * g : 16 * g + 16, 16 * j : 16 * j + 16, :].reshape(256, LANES) for j in range(3)], axis=1
            )
            part = jnp.dot(left, right, preferred_element_type=F32)
            if g == 0:
                acc[...] = part
            else:
                acc[...] += part

        for o in range(8):
            for j in range(3):
                lanes = slice(LANES * j, LANES * j + LANES)
                both = jnp.concatenate([acc[8 * o : 8 * o + 8, lanes], acc[64 + 8 * o : 72 + 8 * o, lanes]], axis=0)
                send3[h, o, 16 * j : 16 * j + 16, :] = both.astype(BF16)

        if h == 0:
            hear_ring()

        def send_owner(i, _):
            o = lax.rem(tile + i, 8)

            @pl.when(jnp.logical_not(stays(o)))
            def _():
                owner_copy(h, o).start()
            return 0

        lax.fori_loop(0, 8, send_owner, 0)

        @pl.when(at_home)
        def _():
            recv3[h, my_source] = send3[h, tile]

    def line_copy(h, i):
        return pltpu.make_async_remote_copy(
            src_ref=line.at[h, z_lo], dst_ref=line.at[h, z_lo], send_sem=sg1_sem.at[h, i], recv_sem=rg1_sem.at[h, z_lo],
            device_id=line_device(i)[1], device_id_type=MESH,
        )

    def finish_mean(h, scale):
        def wait_source(s, _):
            @pl.when(jnp.logical_not(jnp.logical_and(at_home, s == my_source)))
            def _():
                pltpu.make_async_remote_copy(
                    src_ref=send3.at[h, s], dst_ref=recv3.at[h, s],
                    send_sem=send3_sem.at[h, s], recv_sem=recv3_sem.at[h, s],
                    device_id=source_device(s), device_id_type=MESH,
                ).wait_recv()
            return 0

        lax.fori_loop(0, 8, wait_source, 0)
        total = recv3[h, 0].astype(F32)
        for s in range(1, 8):
            total = total + recv3[h, s].astype(F32)
        if h == 0:
            scale = jnp.maximum(total[0:8, :], 1.0)
            total = total[8:48, :]
        mean = [(total[8 * b : 8 * b + 8, :] / scale).astype(BF16).astype(F32) for b in range(5)]

        blank = jnp.zeros((8, LANES), F32)
        pixel = lax.broadcasted_iota(jnp.int32, (LANES, LANES), 0)
        spot = lax.broadcasted_iota(jnp.int32, (LANES, LANES), 1)
        pooled = None
        for g in range(4):
            left = jnp.concatenate([mean[g], mean[4] if g == 0 else blank], axis=0).astype(BF16)
            mix = jnp.where(spot == 32 * g + ((pixel & 63) >> 1), 0.25, 0.0).astype(BF16)
            part = jnp.dot(left, mix, preferred_element_type=F32)
            pooled = part if pooled is None else pooled + part
        line[h, z_lo] = pooled.astype(BF16)

        def send_line(i, _):
            line_copy(h, i).start()
            return 0

        lax.fori_loop(1, 8, send_line, 0)
        comp_ref[40 * h : 40 * h + 40, :] = jnp.concatenate(mean, axis=0)
        return scale

    def plane_device(i):
        xc2 = lax.rem(xc + i, 8)
        return xc2, (z_lo * 8 + xc2, tile)

    def plane_copy(h, i):
        return pltpu.make_async_remote_copy(
            src_ref=line.at[h], dst_ref=rows_ref.at[h, xc], send_sem=sg2_sem.at[h, i], recv_sem=rg2_sem.at[h, xc],
            device_id=plane_device(i)[1], device_id_type=MESH,
        )

    def spread_line(h):
        def wait_line(i, _):
            z2, device = line_device(i)
            pltpu.make_async_remote_copy(
                src_ref=line.at[h, z2], dst_ref=line.at[h, z2], send_sem=sg1_sem.at[h, i], recv_sem=rg1_sem.at[h, z2],
                device_id=device, device_id_type=MESH,
            ).wait_recv()
            return 0

        lax.fori_loop(1, 8, wait_line, 0)

        def send_plane(i, _):
            plane_copy(h, i).start()
            return 0

        lax.fori_loop(1, 8, send_plane, 0)
        rows_ref[h, xc] = line[h]

    reduce_box(0)
    reduce_box(1)
    scale = finish_mean(0, None)
    finish_mean(1, scale)
    spread_line(0)
    spread_line(1)

    for h in range(2):
        def drain_box(i, _, h=h):
            box_copy(h, i, other_core).wait_send()
            return 0

        lax.fori_loop(0, BOX - 1, drain_box, 0)

        def drain_owner(o, _, h=h):
            @pl.when(jnp.logical_not(stays(o)))
            def _():
                owner_copy(h, o).wait_send()
            return 0

        lax.fori_loop(0, 8, drain_owner, 0)

        def wait_plane(i, _, h=h):
            xc2, device = plane_device(i)
            pltpu.make_async_remote_copy(
                src_ref=line.at[h], dst_ref=rows_ref.at[h, xc2], send_sem=sg2_sem.at[h, i], recv_sem=rg2_sem.at[h, xc2],
                device_id=device, device_id_type=MESH,
            ).wait_recv()
            return 0

        lax.fori_loop(1, 8, wait_plane, 0)

        def drain_rows(i, _, h=h):
            line_copy(h, i).wait_send()
            plane_copy(h, i).wait_send()
            return 0

        lax.fori_loop(1, 8, drain_rows, 0)


def exchange(radiance, cloud_weight, footprint):
    any_space = pl.BlockSpec(memory_space=pl.ANY)
    vmem = pl.BlockSpec(memory_space=pltpu.VMEM)
    dma = pltpu.SemaphoreType.DMA
    return pl.pallas_call(
        exchange_kernel,
        out_shape=(
            jax.ShapeDtypeStruct((2, 8, 8, 16, LANES), BF16),
            jax.ShapeDtypeStruct((80, LANES), F32),
        ),
        in_specs=[any_space] * 3,
        out_specs=(vmem, vmem),
        scratch_shapes=[
            pltpu.VMEM((BANDS, K, PIX), BF16),
            pltpu.VMEM((K, PIX), jnp.int32),
            pltpu.VMEM((K, 128), jnp.int32),
            pltpu.VMEM((2, BOX, HALF, LANES), BF16),
            pltpu.VMEM((2, BOX, HALF, LANES), BF16),
            pltpu.VMEM((128, 16 * BOX), BF16),
            pltpu.VMEM((128, 3 * LANES), F32),
            pltpu.VMEM((2, 8, HALF, LANES), BF16),
            pltpu.VMEM((2, 8, HALF, LANES), BF16),
            pltpu.VMEM((2, 8, 16, LANES), BF16),
            pltpu.SemaphoreType.REGULAR((2,)),
            dma((3,)),
            dma((2, BOX)),
            dma((2, BOX)),
            dma((2, 8)),
            dma((2, 8)),
            dma((2, 8)),
            dma((2, 8)),
            dma((2, 8)),
            dma((2, 8)),
        ],
        compiler_params=pltpu.CompilerParams(
            collective_id=0, has_side_effects=True, vmem_limit_bytes=16 * 1024 * 1024
        ),
        name="exchange",
    )(*(pltpu.with_memory_space_constraint(a, pltpu.HBM) for a in (jnp.transpose(radiance, (0, 2, 1, 3)), cloud_weight, footprint.T)))


def pyramid_kernel(rows_ref, comp_ref, composite, one, two, three, four, five, t1, t2, t3):
    composite[...] = comp_ref[...].reshape(BANDS, 8, LANES).astype(BF16)

    before = lax.broadcasted_iota(jnp.int32, (LANES, LANES), 0)
    after = lax.broadcasted_iota(jnp.int32, (LANES, LANES), 1)
    same = (before >> 5) == (after >> 5)
    mix = jnp.where(
        jnp.logical_and(same, ((before & 31) >> 1) == (after & 31)), 0.25, 0.0
    ).astype(BF16)
    unit = jnp.where(before == after, 1.0, 0.0).astype(BF16)

    def halve(values):
        flat = values.reshape(-1, LANES)
        return jnp.dot(flat, mix, preferred_element_type=F32).reshape(values.shape)

    def keep(scratch, row, h, values):
        for i in range(8):
            at = row(i) * 32 + 16 * h
            scratch[at : at + 16, :] = values[i].astype(F32)

    fourth, fifth = [], []
    for h in range(2):
        level = [rows_ref[h, xc] for xc in range(8)]
        for xc in range(8):
            keep(t1, lambda i, xc=xc: i * 8 + xc, h, level[xc])
        for scratch, m in ((t2, 4), (t3, 2), (None, 1)):
            level = [(halve(level[2 * q]) + halve(level[2 * q + 1])).astype(BF16) for q in range(m)]
            if scratch is not None:
                for q in range(m):
                    keep(scratch, lambda i, q=q, m=m: i * m + q, h, level[q])
        fourth.append(level[0].astype(F32))
        last = halve(level[0]).reshape(4, 2, 16, LANES)
        fifth.append((last[:, 0] + last[:, 1]).astype(BF16).astype(F32))

    for scratch, out, height, width in ((t1, one, 64, 32), (t2, two, 32, 16), (t3, three, 16, 8)):
        for r in range(32):
            h, extra, t = r // 16, r // 8 % 2, r % 8
            lines = scratch[pl.ds(r, height, stride=32), :].astype(BF16)
            turned = lax.dot_general(
                unit[0:32] if extra else unit, lines, (((1,), (1,)), ((), ())), preferred_element_type=F32
            )
            for g in range(1 if extra else 4):
                out[t, 5 * h + 4 * extra + g] = turned[32 * g : 32 * g + width].astype(BF16)

    for values, out, height, width in ((fourth, four, 8, 4), (fifth, five, 4, 2)):
        columns = []
        for c in range(width):
            total = None
            for r in range(4):
                h, extra = r // 2, r % 2
                group = before >> 5
                band = 5 * h + 4 if extra else 5 * h + group
                spread = jnp.where(
                    jnp.logical_and(
                        jnp.logical_and((before & 31) == c, after == band), group == 0 if extra else group < 4
                    ),
                    1.0, 0.0,
                ).astype(BF16)
                left = values[h][:, 8 * extra : 8 * extra + 8, :].reshape(8 * height, LANES).astype(BF16)
                part = jnp.dot(left, spread, preferred_element_type=F32)
                total = part if total is None else total + part
            columns.append(total)
        stacked = jnp.concatenate(columns, axis=0).astype(BF16)
        shape = (64 * height, 8 * height * width)
        to = lax.broadcasted_iota(jnp.int32, shape, 0)
        of = lax.broadcasted_iota(jnp.int32, shape, 1)
        high = {8: 3, 4: 2}[height]
        t, r, c = to >> (3 + high), (to >> 3) & (height - 1), to & 7
        order = jnp.where(of == c * (8 * height) + r * 8 + t, 1.0, 0.0).astype(BF16)
        placed = jnp.dot(order, stacked, preferred_element_type=F32)
        for t in range(8):
            for r in range(height):
                at = 8 * (t * height + r)
                out[t, r] = placed[at : at + width, 0:BANDS].astype(BF16)


def pyramid(rows, comp):
    vmem = pl.BlockSpec(memory_space=pltpu.VMEM)
    shapes = [(BANDS, 8, LANES)] + [(8, BANDS, 32 >> i, 64 >> i) for i in range(3)] + [(8, 8, 4, BANDS), (8, 4, 2, BANDS)]
    outs = pl.pallas_call(
        pyramid_kernel,
        out_shape=[jax.ShapeDtypeStruct(s, BF16) for s in shapes],
        in_specs=[vmem] * 2,
        out_specs=[vmem] * 6,
        scratch_shapes=[pltpu.VMEM((32 * (64 >> i), LANES), F32) for i in range(3)],
        compiler_params=pltpu.CompilerParams(vmem_limit_bytes=16 * 1024 * 1024),
        name="pyramid",
    )(rows, comp)
    orders = [(1, 0, 2)] + [(0, 1, 3, 2)] * 3 + [(0, 3, 1, 2)] * 2
    return tuple(jnp.transpose(out, order) for out, order in zip(outs, orders))


def on_device(radiance, cloud_weight, footprint):
    rows, comp = exchange(radiance, cloud_weight, footprint)
    return pyramid(rows, comp)


def solution(mesh):
    in_specs = (P(("scene", "tile"), None, None, None), P(("scene", "tile"), None, None), P())
    out_specs = (
        P("tile", None, "scene"),
        P("tile", None, None, None),
        P("tile", None, None, None),
        P("tile", None, None, None),
        P("tile", None, None, None),
        P("tile", None, None, None),
    )
    return jax.shard_map(
        on_device, mesh=mesh, in_specs=in_specs, out_specs=out_specs, check_vma=False
    )
```

time: 1200 us -> 70.1 us (0.06)
  waiting for transfers between devices: 1050 us -> 0 us
  Pallas kernels: 0 us -> 69.3 us
  local copies, waits for them, and re-layouts: 56.9 us -> 0 us
  starting transfers between devices: 32.4 us -> 0 us
  other arithmetic: 28.9 us -> 0 us
  between operations: 13.9 us -> 0.64 us
  matrix products: 12.2 us -> 0 us
    reduce_scatter x2 -> x0, waiting for transfers between devices: 879 us -> none  [the longest x1 450 us: on_device(): lax.psum_scatter(local_sums, 'scene', scatter_dimension=2, tiled=True)]
    all_gather x1 -> x0, waiting for transfers between devices: 125 us -> none  [on_device(): whole_grid = lax.all_gather(grid, 'scene', axis=2, tiled=True)]
    pallas_call x0 -> x2, Pallas kernels: none -> 69.3 us  [the longest x1 66.2 us: exchange(): pl.pallas_call(exchange_kernel, out_shape=(jax.ShapeDtypeStruct((2, 8, 8,...]
    all_to_all x2 -> x0, waiting for transfers between devices: 47.8 us -> none  [the longest x1 47.7 us: on_device(): lax.all_to_all(send_rad, 'tile', split_axis=0, concat_axis=0, tiled=True)]
    reshape x6 -> x0, local copies, waits for them, and re-layouts: 39.4 us -> none  [the longest x1 25 us: average_pool(): values.astype(jnp.float32)]
    all_to_all x2 -> x0, starting transfers between devices: 32.1 us -> none  [the longest x1 18.3 us: on_device(): lax.all_to_all(send_weight, 'tile', split_axis=0, concat_axis=0, tiled=True)]
    reduce_sum x7 -> x0, other arithmetic: 20.4 us -> none  [the longest x5 20 us: average_pool(): return jnp.mean(shaped, axis=(-3, -1)).astype(jnp.bfloat16)]
    dot_general x5 -> x0, matrix products: 12.2 us -> none  [the longest x1 7.29 us: on_device(): jnp.einsum('scu,scbq->ubq', assign, product, precision=lax.Precision.HIGH...]
  transfers between devices with their start and end apart: 5 -> 0, of which waited for: 5 -> 0; matrix products, arithmetic and copies ran while one was open for 2% -> 0% of each run, Pallas kernels for 0% -> 0%
where the time goes in v2:
time: 70.1 us; the launch traced here: 70 us
  Pallas kernels  69.3 us (99%)
    pallas_call x1, Pallas kernels, exchange(): pl.pallas_call(exchange_kernel, out_shape=(jax.ShapeDtypeStruct((2, 8, 8,...  66.2 us
    pallas_call x1, Pallas kernels, pyramid(): pl.pallas_call(pyramid_kernel, out_shape=[jax.ShapeDtypeStruct(s, BF16) f...  3.12 us

profile of v2, /device:TPU:1, one launch (start us, length us, event | category | flops | bytes accessed | tf_op | source)
XLA Modules:
  0.0 70.0 jit_solution(11812467664867370118)
XLA Ops:
  0.6 66.2 %exchange.1 = (bf16[2,8,8,16,128]{4,3,2,1,0:T(8,128)(2,1)S(1)}, f32[80,128]{1,0:T(8,128)S(1)}) custom-call(bf16[1,10,8,8192]{3,2,1,0:T(8,128)(2,1)} %bitcast.8, s32[1,8,8192]{2,1,0:T(8,128)} %weight_ref.1, s32[8,512]{1,0:T(8,128)} %bitcast.9), custom_call_target="tpu_custom_call" | custom-call | tf_op jit(solution)/shard_map/exchange/pallas_call | solution.py:348
  66.8 3.1 %pyramid.1 = (bf16[10,8,128]{2,1,0:T(8,128)(2,1)}, bf16[8,10,32,64]{3,2,1,0:T(8,128)(2,1)}, bf16[8,10,16,32]{3,2,1,0:T(8,128)(2,1)}, bf16[8,10,8,16]{3,2,1,0:T(8...) custom-call(bf16[2,8,8,16,128]{4,3,2,1,0:T(8,128)(2,1)S(1)} %get-tuple-element.14.rows_ref, ...), custom_call_target="tpu_custom_call" | custom-call | tf_op jit(solution)/shard_map/pyramid/pallas_call | solution.py:464

commit v3 on v2

v3 whole, which is shorter than its diff:
```python
import functools

import jax
import jax.numpy as jnp
from jax import lax
from jax.experimental import pallas as pl
from jax.experimental.pallas import tpu as pltpu
from jax.sharding import PartitionSpec as P

MESH = pl.DeviceIdType.MESH
K = 8
BANDS = 10
TILES = 64
PIX = 8192
LANES = 128
ROWS = (64, 32)
CHUNK = ((0, 7), (7, 10))
BOX = 64
F32 = jnp.float32
BF16 = jnp.bfloat16


STEPS = (
    (2, 2), (2, 1), (1, 2), (2, 3), (3, 2), (2, 0), (1, 1), (0, 2), (3, 3), (1, 3), (3, 1), (1, 0), (0, 1), (3, 0), (0, 3),
)
STEPS_X = sum(step[0] * 4**n for n, step in enumerate(STEPS))
STEPS_Y = sum(step[1] * 4**n for n, step in enumerate(STEPS))


def each_partner(visit):
    def inner(u, carry):
        n, dx, dy = carry
        visit(4 * n + u, dx, dy, 1 - lax.rem(u, 2), 1 - lax.div(u, 2))
        return carry

    def outer(n, carry):
        in_x, in_y = carry
        lax.fori_loop(0, 4, inner, (n, lax.rem(in_x, 4), lax.rem(in_y, 4)))
        return lax.div(in_x, 4), lax.div(in_y, 4)

    lax.fori_loop(0, 15, outer, (jnp.int32(STEPS_X), jnp.int32(STEPS_Y)))
    lax.fori_loop(0, 3, inner, (jnp.int32(15), jnp.int32(0), jnp.int32(0)))


def position():
    scene = lax.axis_index("scene")
    tile = lax.axis_index("tile")
    z_lo = lax.div(scene, 8)
    x = lax.rem(lax.div(scene, 2), 4)
    core = lax.rem(scene, 2)
    z_hi = lax.div(tile, 4)
    y = lax.rem(tile, 4)
    return z_lo, x, core, z_hi, y


def exchange_kernel(
    rad_ref, weight_ref, foot_ref, rows_ref, comp_a, comp_b,
    rad, weight, foot, send_a, send_b, recv_a, recv_b, assign, acc, send3_a, send3_b, recv3_a, recv3_b, mean_a, mean_b, pool, line,
    ring_sem, in_sem, send_sem, recv_sem, send3_sem, recv3_sem, sg1_sem, rg1_sem, sg2_sem, rg2_sem, sc_sem, rc_sem,
):
    send, recv, send3, recv3 = (send_a, send_b), (recv_a, recv_b), (send3_a, send3_b), (recv3_a, recv3_b)
    z_lo, x, core, z_hi, y = position()
    tile = z_hi * 4 + y
    xc = x * 2 + core
    pair = lax.div(z_lo, 2)
    odd = lax.rem(z_lo, 2)

    load_foot = pltpu.make_async_copy(foot_ref.at[:, pl.ds(pl.multiple_of(pair * 128, 128), 128)], foot, in_sem.at[2])
    load_weight = pltpu.make_async_copy(weight_ref.at[0], weight, in_sem.at[1])
    load_rad = pltpu.make_async_copy(rad_ref.at[0], rad, in_sem.at[0])
    load_weight.start()
    load_rad.start()
    load_foot.start()

    def box_device(dx, dy, dc, dz):
        x2 = lax.rem(x + dx, 4)
        y2 = lax.rem(y + dy, 4)
        c2 = lax.rem(core + dc, 2)
        o2 = lax.rem(odd + dz, 2)
        block = (2 * y2 + o2) * 8 + x2 * 2 + c2
        return block, ((2 * pair + o2) * 8 + x2 * 2 + c2, z_hi * 4 + y2)

    ring = z_hi * 4 + pair

    def ring_device(step):
        box = lax.rem(ring + step, 8)
        return ((2 * lax.rem(box, 4) + odd) * 8 + xc, lax.div(box, 4) * 4 + y)

    group = lax.rem(ring + 2, 8)
    home = lax.rem(tile + 6, 8)
    comp, means = (comp_a, comp_b), (mean_a, mean_b)

    def maker_device(j):
        return ((2 * lax.rem(home, 4) + lax.rem(j, 2)) * 8 + xc, lax.div(home, 4) * 4 + lax.div(j, 2))

    my_row = 2 * y + odd
    at_home = group == tile

    barrier = pltpu.get_barrier_semaphore()

    def greet(slot, *offset):
        pl.semaphore_signal(barrier, inc=1, device_id=box_device(*offset)[1], device_id_type=MESH)

    each_partner(greet)
    for step in (1, 7):
        pl.semaphore_signal(barrier, inc=1, device_id=ring_device(step), device_id_type=MESH)

    def tell_ring():
        pl.semaphore_signal(ring_sem.at[0], inc=1, device_id=ring_device(1), device_id_type=MESH)
        pl.semaphore_signal(ring_sem.at[1], inc=1, device_id=ring_device(7), device_id_type=MESH)

    def hear_ring():
        pl.semaphore_wait(ring_sem.at[0], 1)
        pl.semaphore_wait(ring_sem.at[1], 1)

    load_weight.wait()
    load_rad.wait()
    pl.semaphore_wait(barrier, BOX - 1 + 2)
    tell_ring()

    def fill(h, block, out):
        pixels = pl.ds(pl.multiple_of(block * LANES, LANES), LANES)
        w = weight[:, pixels].astype(F32)
        twice = jnp.concatenate([w, w], axis=0).astype(BF16)
        if h == 0:
            first = jnp.concatenate([w, w * rad[0, :, pixels].astype(F32)], axis=0).astype(BF16)
            out[0:16, :] = first
            for j in range(3):
                out[16 * j + 16 : 16 * j + 32, :] = rad[2 * j + 1 : 2 * j + 3, :, pixels].reshape(16, LANES) * twice
        else:
            out[0:16, :] = rad[7:9, :, pixels].reshape(16, LANES) * twice
            last = jnp.concatenate([w * rad[9, :, pixels].astype(F32), jnp.zeros_like(w)], axis=0).astype(BF16)
            out[16:32, :] = last

    def box_copy(h, slot, device):
        return pltpu.make_async_remote_copy(
            src_ref=send[h].at[slot], dst_ref=recv[h].at[slot],
            send_sem=send_sem.at[h, slot], recv_sem=recv_sem.at[h, slot],
            device_id=device, device_id_type=MESH,
        )

    other_core = box_device(0, 0, 1, 0)[1]

    for h in range(2):
        def send_box(slot, *offset, h=h):
            block, device = box_device(*offset)
            fill(h, block, send[h].at[slot])
            box_copy(h, slot, device).start()

        each_partner(send_box)
        fill(h, my_row * 8 + xc, recv[h].at[BOX - 1])
        hear_ring()
        tell_ring()

    load_foot.wait()
    lane = lax.broadcasted_iota(jnp.int32, (1, 16 * BOX), 1)
    slot = lane >> 4
    step = slot >> 2
    dx, dy = jnp.zeros_like(slot), jnp.zeros_like(slot)
    for n, (far_x, far_y) in enumerate(STEPS):
        dx = jnp.where(step == n, far_x, dx)
        dy = jnp.where(step == n, far_y, dy)
    source_row = (
        (((odd + 1 - ((slot >> 1) & 1)) & 1) << 6)
        + (((x - dx) & 3) << 4)
        + (((core + 1 - (slot & 1)) & 1) << 3)
        + ((y - dy) & 3)
        + z_hi * 4
    )
    pick = jnp.where(lax.broadcasted_iota(jnp.int32, (128, 16 * BOX), 0) == source_row, 1.0, 0.0).astype(BF16)
    named = jnp.dot(foot[...].astype(F32).astype(BF16), pick, preferred_element_type=F32)
    own = lax.broadcasted_iota(jnp.int32, (K, 16 * BOX), 0) == (lane & 7)
    target = jnp.sum(jnp.where(own, named, 0.0), axis=0, keepdims=True).astype(jnp.int32) + ((lane & 8) << 3)
    row = lax.broadcasted_iota(jnp.int32, (128, 16 * BOX), 0)
    assign[...] = jnp.where(row == target, 1.0, 0.0).astype(BF16)
    hear_ring()
    tell_ring()

    def ring_copy(h, i):
        return pltpu.make_async_remote_copy(
            src_ref=send3[h].at[lax.rem(group + i, 8)], dst_ref=recv3[h].at[ring],
            send_sem=send3_sem.at[h, i], recv_sem=recv3_sem.at[h, ring],
            device_id=ring_device(i), device_id_type=MESH,
        )

    def reduce_box(h):
        def wait_box(i, _):
            box_copy(h, i, other_core).wait_recv()
            return 0

        for g in range(4):
            lax.fori_loop(16 * g, min(16 * g + 16, BOX - 1), wait_box, 0)
            left = assign[:, 256 * g : 256 * g + 256]
            right = jnp.concatenate(
                [recv[h][16 * g : 16 * g + 16, 16 * j : 16 * j + 16, :].reshape(256, LANES) for j in range(ROWS[h] // 16)],
                axis=1,
            )
            part = jnp.dot(left, right, preferred_element_type=F32)
            if g == 0:
                acc[:, 0 : 8 * ROWS[h]] = part
            else:
                acc[:, 0 : 8 * ROWS[h]] += part

        for o in range(8):
            for j in range(ROWS[h] // 16):
                lanes = slice(LANES * j, LANES * j + LANES)
                both = jnp.concatenate([acc[8 * o : 8 * o + 8, lanes], acc[64 + 8 * o : 72 + 8 * o, lanes]], axis=0)
                send3[h][o, 16 * j : 16 * j + 16, :] = both.astype(BF16)

        if h == 0:
            hear_ring()

        def send_ring(i, _):
            ring_copy(h, i).start()
            return 0

        lax.fori_loop(1, 8, send_ring, 0)
        recv3[h][ring] = send3[h][group]

    def line_copy(h, z2):
        return pltpu.make_async_remote_copy(
            src_ref=pool.at[h], dst_ref=line.at[h, my_row], send_sem=sg1_sem.at[h, z2], recv_sem=rg1_sem.at[h, my_row],
            device_id=(z2 * 8 + xc, group), device_id_type=MESH,
        )

    def comp_copy(h):
        return pltpu.make_async_remote_copy(
            src_ref=means[h], dst_ref=comp[h], send_sem=sc_sem.at[h], recv_sem=rc_sem.at[h],
            device_id=(my_row * 8 + xc, group), device_id_type=MESH,
        )

    def stays(z2):
        return jnp.logical_and(at_home, z2 == z_lo)

    def finish_mean(h, scale):
        def wait_ring(i, _):
            s = lax.rem(ring + i, 8)
            pltpu.make_async_remote_copy(
                src_ref=send3[h].at[s], dst_ref=recv3[h].at[s],
                send_sem=send3_sem.at[h, i], recv_sem=recv3_sem.at[h, s],
                device_id=ring_device(i), device_id_type=MESH,
            ).wait_recv()
            return 0

        lax.fori_loop(1, 8, wait_ring, 0)
        total = recv3[h][0].astype(F32)
        for s in range(1, 8):
            total = total + recv3[h][s].astype(F32)
        if h == 0:
            scale = jnp.maximum(total[0:8, :], 1.0)
            total = total[8:64, :]
        first, end = CHUNK[h]
        bands = end - first
        mean = [(total[8 * b : 8 * b + 8, :] / scale).astype(BF16).astype(F32) for b in range(bands)]

        blank = jnp.zeros((8, LANES), F32)
        pixel = lax.broadcasted_iota(jnp.int32, (LANES, LANES), 0)
        spot = lax.broadcasted_iota(jnp.int32, (LANES, LANES), 1)
        pooled = None
        for g in range(min(4, bands)):
            left = jnp.concatenate([mean[g], mean[4 + g] if 4 + g < bands else blank], axis=0).astype(BF16)
            mix = jnp.where(spot == 32 * g + ((pixel & 63) >> 1), 0.25, 0.0).astype(BF16)
            part = jnp.dot(left, mix, preferred_element_type=F32)
            pooled = part if pooled is None else pooled + part
        pool[h] = pooled.astype(BF16)

        def send_line(z2, _):
            @pl.when(jnp.logical_not(stays(z2)))
            def _():
                line_copy(h, z2).start()
            return 0

        lax.fori_loop(0, 8, send_line, 0)
        means[h][...] = jnp.concatenate(mean[0:bands] + [blank], axis=0).astype(BF16)

        @pl.when(jnp.logical_not(stays(my_row)))
        def _():
            comp_copy(h).start()

        @pl.when(stays(my_row))
        def _():
            comp[h][...] = means[h][...]

        @pl.when(at_home)
        def _():
            line[h, my_row] = pool[h]
        return scale

    def plane_device(i):
        xc2 = lax.rem(xc + i, 8)
        return xc2, (z_lo * 8 + xc2, tile)

    def plane_copy(h, i):
        return pltpu.make_async_remote_copy(
            src_ref=line.at[h], dst_ref=rows_ref.at[h, xc], send_sem=sg2_sem.at[h, i], recv_sem=rg2_sem.at[h, xc],
            device_id=plane_device(i)[1], device_id_type=MESH,
        )

    def spread_line(h):
        def wait_line(j, _):
            @pl.when(jnp.logical_not(jnp.logical_and(at_home, j == my_row)))
            def _():
                pltpu.make_async_remote_copy(
                    src_ref=pool.at[h], dst_ref=line.at[h, j], send_sem=sg1_sem.at[h, j], recv_sem=rg1_sem.at[h, j],
                    device_id=maker_device(j), device_id_type=MESH,
                ).wait_recv()
            return 0

        lax.fori_loop(0, 8, wait_line, 0)

        def send_plane(i, _):
            plane_copy(h, i).start()
            return 0

        lax.fori_loop(1, 8, send_plane, 0)
        rows_ref[h, xc] = line[h]

    reduce_box(0)
    reduce_box(1)
    scale = finish_mean(0, None)
    finish_mean(1, scale)
    spread_line(0)
    spread_line(1)

    for h in range(2):
        def drain_box(i, _, h=h):
            box_copy(h, i, other_core).wait_send()
            return 0

        lax.fori_loop(0, BOX - 1, drain_box, 0)

        def drain_ring(i, _, h=h):
            ring_copy(h, i).wait_send()
            return 0

        lax.fori_loop(1, 8, drain_ring, 0)

        @pl.when(jnp.logical_not(stays(my_row)))
        def _(h=h):
            comp_copy(h).wait_send()

        @pl.when(jnp.logical_not(jnp.logical_and(at_home, my_row == z_lo)))
        def _(h=h):
            pltpu.make_async_remote_copy(
                src_ref=means[h], dst_ref=comp[h], send_sem=sc_sem.at[h], recv_sem=rc_sem.at[h],
                device_id=maker_device(z_lo), device_id_type=MESH,
            ).wait_recv()

        def drain_line(z2, _, h=h):
            @pl.when(jnp.logical_not(stays(z2)))
            def _():
                line_copy(h, z2).wait_send()
            return 0

        lax.fori_loop(0, 8, drain_line, 0)

        def wait_plane(i, _, h=h):
            xc2, device = plane_device(i)
            pltpu.make_async_remote_copy(
                src_ref=line.at[h], dst_ref=rows_ref.at[h, xc2], send_sem=sg2_sem.at[h, i], recv_sem=rg2_sem.at[h, xc2],
                device_id=device, device_id_type=MESH,
            ).wait_recv()
            return 0

        lax.fori_loop(1, 8, wait_plane, 0)

        def drain_rows(i, _, h=h):
            plane_copy(h, i).wait_send()
            return 0

        lax.fori_loop(1, 8, drain_rows, 0)


def exchange(radiance, cloud_weight, footprint):
    any_space = pl.BlockSpec(memory_space=pl.ANY)
    vmem = pl.BlockSpec(memory_space=pltpu.VMEM)
    dma = pltpu.SemaphoreType.DMA
    return pl.pallas_call(
        exchange_kernel,
        out_shape=(
            jax.ShapeDtypeStruct((2, 8, 8, 16, LANES), BF16),
            *(jax.ShapeDtypeStruct((rows, LANES), BF16) for rows in ROWS),
        ),
        in_specs=[any_space] * 3,
        out_specs=(vmem, vmem, vmem),
        scratch_shapes=[
            pltpu.VMEM((BANDS, K, PIX), BF16),
            pltpu.VMEM((K, PIX), jnp.int32),
            pltpu.VMEM((K, 128), jnp.int32),
            *(pltpu.VMEM((BOX, rows, LANES), BF16) for rows in ROWS * 2),
            pltpu.VMEM((128, 16 * BOX), BF16),
            pltpu.VMEM((128, 4 * LANES), F32),
            *(pltpu.VMEM((8, rows, LANES), BF16) for rows in ROWS * 2),
            *(pltpu.VMEM((rows, LANES), BF16) for rows in ROWS),
            pltpu.VMEM((2, 16, LANES), BF16),
            pltpu.VMEM((2, 8, 16, LANES), BF16),
            pltpu.SemaphoreType.REGULAR((2,)),
            dma((3,)),
            dma((2, BOX)),
            dma((2, BOX)),
            dma((2, 8)),
            dma((2, 8)),
            dma((2, 8)),
            dma((2, 8)),
            dma((2, 8)),
            dma((2, 8)),
            dma((2,)),
            dma((2,)),
        ],
        compiler_params=pltpu.CompilerParams(
            collective_id=0, has_side_effects=True, vmem_limit_bytes=16 * 1024 * 1024
        ),
        name="exchange",
    )(*(pltpu.with_memory_space_constraint(a, pltpu.HBM) for a in (jnp.transpose(radiance, (0, 2, 1, 3)), cloud_weight, footprint.T)))


GROUPS = ((0, 0, 0, 4), (0, 8, 4, 3), (1, 0, 7, 3))


def pyramid_kernel(rows_ref, comp_a, comp_b, *refs):
    outs, (composite, one, two, three, four, five), (t1, t2, t3), sems = refs[:6], refs[6:12], refs[12:15], refs[15]

    def put(i):
        return pltpu.make_async_copy(refs[6 + i], outs[i], sems.at[i])

    before = lax.broadcasted_iota(jnp.int32, (LANES, LANES), 0)
    after = lax.broadcasted_iota(jnp.int32, (LANES, LANES), 1)
    same = (before >> 5) == (after >> 5)
    mix = jnp.where(
        jnp.logical_and(same, ((before & 31) >> 1) == (after & 31)), 0.25, 0.0
    ).astype(BF16)
    unit = jnp.where(before == after, 1.0, 0.0).astype(BF16)

    def halve(values):
        flat = values.reshape(-1, LANES)
        return jnp.dot(flat, mix, preferred_element_type=F32).reshape(values.shape)

    def keep(scratch, row, h, values):
        for i in range(8):
            at = row(i) * 24 + 16 * h
            lines = 8 if h else 16
            scratch[at : at + lines, :] = values[i].astype(F32)[0:lines]

    def turn(scratch, out, height, width):
        for r in range(24):
            _, _, first, bands = GROUPS[r // 8]
            lines = scratch[pl.ds(r, height, stride=24), :].astype(BF16)
            turned = lax.dot_general(
                unit[0 : 32 * bands], lines, (((1,), (1,)), ((), ())), preferred_element_type=F32
            )
            for g in range(bands):
                out[r % 8, first + g] = turned[32 * g : 32 * g + width].astype(BF16)

    level = [[rows_ref[h, xc] for xc in range(8)] for h in range(2)]
    for h in range(2):
        for xc in range(8):
            keep(t1, lambda i, xc=xc: i * 8 + xc, h, level[h][xc])
    turn(t1, one, 64, 32)
    put(1).start()
    for comp, (first, end) in zip((comp_a, comp_b), CHUNK):
        lines = comp[...].astype(F32)[0 : 8 * (end - first)]
        composite[first:end] = lines.reshape(end - first, 8, LANES).astype(BF16)
    put(0).start()
    for scratch, out, m in ((t2, two, 4), (t3, three, 2), (None, None, 1)):
        for h in range(2):
            level[h] = [(halve(level[h][2 * q]) + halve(level[h][2 * q + 1])).astype(BF16) for q in range(m)]
            if scratch is not None:
                for q in range(m):
                    keep(scratch, lambda i, q=q, m=m: i * m + q, h, level[h][q])
        if scratch is not None:
            turn(scratch, out, 8 * m, 4 * m)
            put(2 if m == 4 else 3).start()
    fourth, fifth = [], []
    for h in range(2):
        fourth.append(level[h][0].astype(F32))
        last = halve(level[h][0]).reshape(4, 2, 16, LANES)
        fifth.append((last[:, 0] + last[:, 1]).astype(BF16).astype(F32))

    for values, out, height, width in ((fourth, four, 8, 4), (fifth, five, 4, 2)):
        columns = []
        for c in range(width):
            total = None
            for h, line, first, bands in GROUPS:
                group = before >> 5
                spread = jnp.where(
                    jnp.logical_and(
                        jnp.logical_and((before & 31) == c, after == first + group), group < bands
                    ),
                    1.0, 0.0,
                ).astype(BF16)
                left = values[h][:, line : line + 8, :].reshape(8 * height, LANES).astype(BF16)
                part = jnp.dot(left, spread, preferred_element_type=F32)
                total = part if total is None else total + part
            columns.append(total)
        stacked = jnp.concatenate(columns, axis=0).astype(BF16)
        shape = (64 * height, 8 * height * width)
        to = lax.broadcasted_iota(jnp.int32, shape, 0)
        of = lax.broadcasted_iota(jnp.int32, shape, 1)
        high = {8: 3, 4: 2}[height]
        t, r, c = to >> (3 + high), (to >> 3) & (height - 1), to & 7
        order = jnp.where(of == c * (8 * height) + r * 8 + t, 1.0, 0.0).astype(BF16)
        placed = jnp.dot(order, stacked, preferred_element_type=F32)
        for t in range(8):
            for r in range(height):
                at = 8 * (t * height + r)
                out[t, r] = placed[at : at + width, 0:BANDS].astype(BF16)
        put(4 if height == 8 else 5).start()
    for i in range(6):
        put(i).wait()


def pyramid(rows, comp_a, comp_b):
    vmem = pl.BlockSpec(memory_space=pltpu.VMEM)
    shapes = [(BANDS, 8, LANES)] + [(8, BANDS, 32 >> i, 64 >> i) for i in range(3)] + [(8, 8, 4, BANDS), (8, 4, 2, BANDS)]
    outs = pl.pallas_call(
        pyramid_kernel,
        out_shape=[jax.ShapeDtypeStruct(s, BF16) for s in shapes],
        in_specs=[vmem] * 3,
        out_specs=[pl.BlockSpec(memory_space=pl.ANY)] * 6,
        scratch_shapes=[pltpu.VMEM(s, BF16) for s in shapes]
        + [pltpu.VMEM((24 * (64 >> i), LANES), F32) for i in range(3)]
        + [pltpu.SemaphoreType.DMA((6,))],
        compiler_params=pltpu.CompilerParams(vmem_limit_bytes=16 * 1024 * 1024),
        name="pyramid",
    )(rows, comp_a, comp_b)
    orders = [(1, 0, 2)] + [(0, 1, 3, 2)] * 3 + [(0, 3, 1, 2)] * 2
    return tuple(jnp.transpose(out, order) for out, order in zip(outs, orders))


def on_device(radiance, cloud_weight, footprint):
    return pyramid(*exchange(radiance, cloud_weight, footprint))


def solution(mesh):
    in_specs = (P(("scene", "tile"), None, None, None), P(("scene", "tile"), None, None), P())
    out_specs = (
        P("tile", None, "scene"),
        P("tile", None, None, None),
        P("tile", None, None, None),
        P("tile", None, None, None),
        P("tile", None, None, None),
        P("tile", None, None, None),
    )
    return jax.shard_map(
        on_device, mesh=mesh, in_specs=in_specs, out_specs=out_specs, check_vma=False
    )
```

time: 70.1 us -> 66.3 us (0.946)
  Pallas kernels: 69.3 us -> 65.6 us
    pallas_call x1, Pallas kernels: 66.2 us -> 63.2 us  [exchange(): pl.pallas_call(exchange_kernel, out_shape=(jax.ShapeDtypeStruct((2, 8, 8,...]
where the time goes in v3:
time: 66.3 us; the launch traced here: 66.2 us
  Pallas kernels  65.6 us (99%)
    pallas_call x1, Pallas kernels, exchange(): pl.pallas_call(exchange_kernel, out_shape=(jax.ShapeDtypeStruct((2, 8, 8,...  63.2 us
    pallas_call x1, Pallas kernels, pyramid(): pl.pallas_call(pyramid_kernel, out_shape=[jax.ShapeDtypeStruct(s, BF16) f...  2.42 us

profile of v3, /device:TPU:1, one launch (start us, length us, event | category | flops | bytes accessed | tf_op | source)
XLA Modules:
  0.0 66.2 jit_solution(12797326353137118618)
XLA Ops:
  0.6 63.2 %exchange.1 = (bf16[2,8,8,16,128]{4,3,2,1,0:T(8,128)(2,1)S(1)}, bf16[64,128]{1,0:T(8,128)(2,1)S(1)}, bf16[32,128]{1,0:T(8,128)(2,1)S(1)}) custom-call(bf16[1,10,8,8192]{3,2,1,0:T(8,128)(2,1)} %bitcast.8, s32[1,8,8192]{2,1,0:T(8,128)} %weight_ref.1, s32[8,512]{1,0:T(8,128)} %bitcast.9), custom_call_target="tpu_custom_call" | custom-call | tf_op jit(solution)/shard_map/exchange/pallas_call | solution.py:378
  63.8 2.4 %pyramid.1 = (bf16[10,8,128]{2,1,0:T(8,128)(2,1)}, bf16[8,10,32,64]{3,2,1,0:T(8,128)(2,1)}, bf16[8,10,16,32]{3,2,1,0:T(8,128)(2,1)}, bf16[8,10,8,16]{3,2,1,0:T(8...) custom-call(bf16[2,8,8,16,128]{4,3,2,1,0:T(8,128)(2,1)S(1)} %get-tuple-element.15.rows_ref, ...), custom_call_target="tpu_custom_call" | custom-call | tf_op jit(solution)/shard_map/pyramid/pallas_call | solution.py:515

commit v4 on v3

--- a/solution.py
+++ b/solution.py
@@ -14,7 +14,8 @@
 PIX = 8192
 LANES = 128
 ROWS = (64, 32)
-CHUNK = ((0, 7), (7, 10))
+SHORT = 48
+CHUNK = ((0, 6), (6, 10))
 BOX = 64
 F32 = jnp.float32
 BF16 = jnp.bfloat16
@@ -27,19 +28,46 @@
 STEPS_Y = sum(step[1] * 4**n for n, step in enumerate(STEPS))
 
 
-def each_partner(visit):
-    def inner(u, carry):
-        n, dx, dy = carry
-        visit(4 * n + u, dx, dy, 1 - lax.rem(u, 2), 1 - lax.div(u, 2))
-        return carry
-
-    def outer(n, carry):
-        in_x, in_y = carry
-        lax.fori_loop(0, 4, inner, (n, lax.rem(in_x, 4), lax.rem(in_y, 4)))
-        return lax.div(in_x, 4), lax.div(in_y, 4)
-
-    lax.fori_loop(0, 15, outer, (jnp.int32(STEPS_X), jnp.int32(STEPS_Y)))
-    lax.fori_loop(0, 3, inner, (jnp.int32(15), jnp.int32(0), jnp.int32(0)))
+GROUPS = (((0, 4), (4, 2)), ((6, 4),))
+
+
+def matrices():
+    before = lax.broadcasted_iota(jnp.int32, (LANES, LANES), 0)
+    after = lax.broadcasted_iota(jnp.int32, (LANES, LANES), 1)
+    same = (before >> 5) == (after >> 5)
+    mix = jnp.where(jnp.logical_and(same, ((before & 31) >> 1) == (after & 31)), 0.25, 0.0).astype(BF16)
+    unit = jnp.where(before == after, 1.0, 0.0).astype(BF16)
+    return before, after, mix, unit
+
+
+def halve(values, mix):
+    flat = values.reshape(-1, LANES).astype(BF16)
+    return jnp.dot(flat, mix, preferred_element_type=F32).reshape(values.shape)
+
+
+def overviews(h, level, mix, unit, scratches, outs, done):
+    lines = 8 * len(GROUPS[h])
+    base = CHUNK[h][0]
+    for depth in range(4):
+        m = 8 >> depth
+        if depth:
+            level = [(halve(level[2 * q], mix) + halve(level[2 * q + 1], mix)).astype(BF16).astype(F32) for q in range(m)]
+        if depth == 3:
+            return level[0]
+        scratch, out = scratches[depth], outs[depth]
+        for q in range(m):
+            for i in range(8):
+                at = (i * m + q) * lines
+                scratch[at : at + lines, :] = level[q][i]
+        for r in range(lines):
+            first, bands = GROUPS[h][r // 8]
+            picked = scratch[pl.ds(r, 8 * m, stride=lines), :].astype(BF16)
+            turned = lax.dot_general(
+                unit[0 : 32 * bands], picked, (((1,), (1,)), ((), ())), preferred_element_type=F32
+            )
+            for g in range(bands):
+                out[r % 8, first - base + g] = turned[32 * g : 32 * g + 4 * m].astype(BF16)
+        done(depth)
 
 
 def position():
@@ -54,9 +82,9 @@
 
 
 def exchange_kernel(
-    rad_ref, weight_ref, foot_ref, rows_ref, comp_a, comp_b,
-    rad, weight, foot, send_a, send_b, recv_a, recv_b, assign, acc, send3_a, send3_b, recv3_a, recv3_b, mean_a, mean_b, pool, line,
-    ring_sem, in_sem, send_sem, recv_sem, send3_sem, recv3_sem, sg1_sem, rg1_sem, sg2_sem, rg2_sem, sc_sem, rc_sem,
+    rad_ref, weight_ref, foot_ref, rows_b, one, two, three, fourth, comp_a, comp_b,
+    rad, weight, foot, send_a, send_b, recv_a, recv_b, assign, acc, send3_a, send3_b, recv3_a, recv3_b, mean_a, mean_b, pool, swap_out, swap_in, line, packed, rows_a, t1, t2, t3,
+    ring_sem, in_sem, send_sem, recv_sem, send3_sem, recv3_sem, sg1_sem, rg1_sem, sg2_sem, rg2_sem, sc_sem, rc_sem, swap_sem,
 ):
     send, recv, send3, recv3 = (send_a, send_b), (recv_a, recv_b), (send3_a, send3_b), (recv3_a, recv3_b)
     z_lo, x, core, z_hi, y = position()
@@ -72,13 +100,22 @@
     load_rad.start()
     load_foot.start()
 
-    def box_device(dx, dy, dc, dz):
-        x2 = lax.rem(x + dx, 4)
-        y2 = lax.rem(y + dy, 4)
-        c2 = lax.rem(core + dc, 2)
-        o2 = lax.rem(odd + dz, 2)
+    def box_device(x2, y2, c2, o2):
         block = (2 * y2 + o2) * 8 + x2 * 2 + c2
         return block, ((2 * pair + o2) * 8 + x2 * 2 + c2, z_hi * 4 + y2)
+
+    def each_partner(visit):
+        def four(n, x2, y2, count):
+            for u in range(count):
+                visit(4 * n + u, u % 2, x2, y2, core if u % 2 else 1 - core, odd if u // 2 else 1 - odd)
+
+        def outer(n, carry):
+            in_x, in_y = carry
+            four(n, lax.rem(x + lax.rem(in_x, 4), 4), lax.rem(y + lax.rem(in_y, 4), 4), 4)
+            return lax.div(in_x, 4), lax.div(in_y, 4)
+
+        lax.fori_loop(0, 15, outer, (jnp.int32(STEPS_X), jnp.int32(STEPS_Y)))
+        four(15, x, y, 3)
 
     ring = z_hi * 4 + pair
 
@@ -89,6 +126,7 @@
     group = lax.rem(ring + 2, 8)
     home = lax.rem(tile + 6, 8)
     comp, means = (comp_a, comp_b), (mean_a, mean_b)
+    whole_line, rows = (line.at[0], packed), (rows_a, rows_b)
 
     def maker_device(j):
         return ((2 * lax.rem(home, 4) + lax.rem(j, 2)) * 8 + xc, lax.div(home, 4) * 4 + lax.div(j, 2))
@@ -98,10 +136,16 @@
 
     barrier = pltpu.get_barrier_semaphore()
 
-    def greet(slot, *offset):
+    def greet(slot, same, *offset):
         pl.semaphore_signal(barrier, inc=1, device_id=box_device(*offset)[1], device_id_type=MESH)
 
     each_partner(greet)
+
+    def clear(n, _):
+        recv_a[2 * n, SHORT:64] = jnp.zeros((16, LANES), BF16)
+        return 0
+
+    lax.fori_loop(0, BOX // 2, clear, 0)
     for step in (1, 7):
         pl.semaphore_signal(barrier, inc=1, device_id=ring_device(step), device_id_type=MESH)
 
@@ -118,37 +162,54 @@
     pl.semaphore_wait(barrier, BOX - 1 + 2)
     tell_ring()
 
-    def fill(h, block, out):
+    def fill(h, same, block, out):
         pixels = pl.ds(pl.multiple_of(block * LANES, LANES), LANES)
         w = weight[:, pixels].astype(F32)
         twice = jnp.concatenate([w, w], axis=0).astype(BF16)
-        if h == 0:
-            first = jnp.concatenate([w, w * rad[0, :, pixels].astype(F32)], axis=0).astype(BF16)
-            out[0:16, :] = first
-            for j in range(3):
-                out[16 * j + 16 : 16 * j + 32, :] = rad[2 * j + 1 : 2 * j + 3, :, pixels].reshape(16, LANES) * twice
-        else:
-            out[0:16, :] = rad[7:9, :, pixels].reshape(16, LANES) * twice
-            last = jnp.concatenate([w * rad[9, :, pixels].astype(F32), jnp.zeros_like(w)], axis=0).astype(BF16)
-            out[16:32, :] = last
-
-    def box_copy(h, slot, device):
+        if h == 1:
+            for j in range(2):
+                out[16 * j : 16 * j + 16, :] = rad[2 * j + 6 : 2 * j + 8, :, pixels].reshape(16, LANES) * twice
+            return
+        first = jnp.concatenate([w, w * rad[0, :, pixels].astype(F32)], axis=0).astype(BF16)
+        out[0:16, :] = first
+        for j in range(2):
+            out[16 * j + 16 : 16 * j + 32, :] = rad[2 * j + 1 : 2 * j + 3, :, pixels].reshape(16, LANES) * twice
+        if same:
+            beside = pl.ds(pl.multiple_of((block + 1 - 2 * core) * LANES, LANES), LANES)
+            mine = w * rad[5, :, pixels].astype(F32)
+            theirs = weight[:, beside].astype(F32) * rad[5, :, beside].astype(F32)
+            out[48:64, :] = jnp.concatenate([mine, theirs], axis=0).astype(BF16)
+
+    def box_copy(h, same, slot, device):
+        source, target = send[h].at[slot], recv[h].at[slot]
+        if h == 0 and not same:
+            source, target = send[h].at[slot, 0:SHORT], recv[h].at[slot, 0:SHORT]
         return pltpu.make_async_remote_copy(
-            src_ref=send[h].at[slot], dst_ref=recv[h].at[slot],
+            src_ref=source, dst_ref=target,
             send_sem=send_sem.at[h, slot], recv_sem=recv_sem.at[h, slot],
             device_id=device, device_id_type=MESH,
         )
 
-    other_core = box_device(0, 0, 1, 0)[1]
+    def each_pair(first, end, visit):
+        def pair_of(n, _):
+            visit(2 * n, 0)
+            visit(2 * n + 1, 1)
+            return 0
+
+        lax.fori_loop(first // 2, end // 2, pair_of, 0)
+        if end % 2:
+            visit(end - 1, 0)
+
+    other_core = box_device(x, y, 1 - core, odd)[1]
 
     for h in range(2):
-        def send_box(slot, *offset, h=h):
+        def send_box(slot, same, *offset, h=h):
             block, device = box_device(*offset)
-            fill(h, block, send[h].at[slot])
-            box_copy(h, slot, device).start()
+            fill(h, same, block, send[h].at[slot])
+            box_copy(h, same, slot, device).start()
 
         each_partner(send_box)
-        fill(h, my_row * 8 + xc, recv[h].at[BOX - 1])
+        fill(h, 1, my_row * 8 + xc, recv[h].at[BOX - 1])
         hear_ring()
         tell_ring()
 
@@ -184,12 +245,11 @@
         )
 
     def reduce_box(h):
-        def wait_box(i, _):
-            box_copy(h, i, other_core).wait_recv()
-            return 0
+        def wait_box(slot, same):
+            box_copy(h, same, slot, other_core).wait_recv()
 
         for g in range(4):
-            lax.fori_loop(16 * g, min(16 * g + 16, BOX - 1), wait_box, 0)
+            each_pair(16 * g, min(16 * g + 16, BOX - 1), wait_box)
             left = assign[:, 256 * g : 256 * g + 256]
             right = jnp.concatenate(
                 [recv[h][16 * g : 16 * g + 16, 16 * j : 16 * j + 16, :].reshape(256, LANES) for j in range(ROWS[h] // 16)],
@@ -229,6 +289,12 @@
             device_id=(my_row * 8 + xc, group), device_id_type=MESH,
         )
 
+    def swap_copy():
+        return pltpu.make_async_remote_copy(
+            src_ref=swap_out, dst_ref=swap_in, send_sem=swap_sem.at[0], recv_sem=swap_sem.at[1],
+            device_id=other_core, device_id_type=MESH,
+        )
+
     def stays(z2):
         return jnp.logical_and(at_home, z2 == z_lo)
 
@@ -247,8 +313,12 @@
         for s in range(1, 8):
             total = total + recv3[h][s].astype(F32)
         if h == 0:
+            swap_out[...] = jnp.concatenate([total[56:64], jnp.zeros((8, LANES), F32)], axis=0).astype(BF16)
+            swap_copy().start()
             scale = jnp.maximum(total[0:8, :], 1.0)
-            total = total[8:64, :]
+            swap_copy().wait_recv()
+            split = total[48:56, :] + swap_in[...].astype(F32)[0:8]
+            total = jnp.concatenate([total[8:48, :], split], axis=0)
         first, end = CHUNK[h]
         bands = end - first
         mean = [(total[8 * b : 8 * b + 8, :] / scale).astype(BF16).astype(F32) for b in range(bands)]
@@ -271,7 +341,8 @@
             return 0
 
         lax.fori_loop(0, 8, send_line, 0)
-        means[h][...] = jnp.concatenate(mean[0:bands] + [blank], axis=0).astype(BF16)
+        spare = ROWS[h] // 8 - bands
+        means[h][...] = jnp.concatenate(mean[0:bands] + [blank] * spare, axis=0).astype(BF16)
 
         @pl.when(jnp.logical_not(stays(my_row)))
         def _():
@@ -292,7 +363,7 @@
 
     def plane_copy(h, i):
         return pltpu.make_async_remote_copy(
-            src_ref=line.at[h], dst_ref=rows_ref.at[h, xc], send_sem=sg2_sem.at[h, i], recv_sem=rg2_sem.at[h, xc],
+            src_ref=whole_line[h], dst_ref=rows[h].at[xc], send_sem=sg2_sem.at[h, i], recv_sem=rg2_sem.at[h, xc],
             device_id=plane_device(i)[1], device_id_type=MESH,
         )
 
@@ -307,13 +378,17 @@
             return 0
 
         lax.fori_loop(0, 8, wait_line, 0)
+        if h == 1:
+            for q in range(4):
+                both = [line[1, 2 * q + i].astype(F32)[0:8] for i in range(2)]
+                packed[16 * q : 16 * q + 16, :] = jnp.concatenate(both, axis=0).astype(BF16)
 
         def send_plane(i, _):
             plane_copy(h, i).start()
             return 0
 
         lax.fori_loop(1, 8, send_plane, 0)
-        rows_ref[h, xc] = line[h]
+        rows[h][xc] = whole_line[h][...]
 
     reduce_box(0)
     reduce_box(1)
@@ -323,11 +398,26 @@
     spread_line(1)
 
     for h in range(2):
-        def drain_box(i, _, h=h):
-            box_copy(h, i, other_core).wait_send()
-            return 0
-
-        lax.fori_loop(0, BOX - 1, drain_box, 0)
+        def wait_plane(i, _, h=h):
+            xc2, device = plane_device(i)
+            pltpu.make_async_remote_copy(
+                src_ref=whole_line[h], dst_ref=rows[h].at[xc2], send_sem=sg2_sem.at[h, i], recv_sem=rg2_sem.at[h, xc2],
+                device_id=device, device_id_type=MESH,
+            ).wait_recv()
+            return 0
+
+        lax.fori_loop(1, 8, wait_plane, 0)
+        if h == 0:
+            _, _, mix, unit = matrices()
+            level = [rows_a[i].astype(F32) for i in range(8)]
+            fourth[...] = overviews(0, level, mix, unit, (t1, t2, t3), (one, two, three), lambda depth: None)
+
+    swap_copy().wait_send()
+    for h in range(2):
+        def drain_box(slot, same, h=h):
+            box_copy(h, same, slot, other_core).wait_send()
+
+        each_pair(0, BOX - 1, drain_box)
 
         def drain_ring(i, _, h=h):
             ring_copy(h, i).wait_send()
@@ -353,16 +443,6 @@
             return 0
 
         lax.fori_loop(0, 8, drain_line, 0)
-
-        def wait_plane(i, _, h=h):
-            xc2, device = plane_device(i)
-            pltpu.make_async_remote_copy(
-                src_ref=line.at[h], dst_ref=rows_ref.at[h, xc2], send_sem=sg2_sem.at[h, i], recv_sem=rg2_sem.at[h, xc2],
-                device_id=device, device_id_type=MESH,
-            ).wait_recv()
-            return 0
-
-        lax.fori_loop(1, 8, wait_plane, 0)
 
         def drain_rows(i, _, h=h):
             plane_copy(h, i).wait_send()
@@ -378,11 +458,13 @@
     return pl.pallas_call(
         exchange_kernel,
         out_shape=(
-            jax.ShapeDtypeStruct((2, 8, 8, 16, LANES), BF16),
+            jax.ShapeDtypeStruct((8, 64, LANES), BF16),
+            *(jax.ShapeDtypeStruct((8, CHUNK[0][1], 32 >> i, 64 >> i), BF16) for i in range(3)),
+            jax.ShapeDtypeStruct((8, 16, LANES), F32),
             *(jax.ShapeDtypeStruct((rows, LANES), BF16) for rows in ROWS),
         ),
         in_specs=[any_space] * 3,
-        out_specs=(vmem, vmem, vmem),
+        out_specs=(vmem,) * 7,
         scratch_shapes=[
             pltpu.VMEM((BANDS, K, PIX), BF16),
             pltpu.VMEM((K, PIX), jnp.int32),
@@ -392,8 +474,11 @@
             pltpu.VMEM((128, 4 * LANES), F32),
             *(pltpu.VMEM((8, rows, LANES), BF16) for rows in ROWS * 2),
             *(pltpu.VMEM((rows, LANES), BF16) for rows in ROWS),
-            pltpu.VMEM((2, 16, LANES), BF16),
+            *(pltpu.VMEM(shape, BF16) for shape in ((2, 16, LANES), (16, LANES), (16, LANES))),
             pltpu.VMEM((2, 8, 16, LANES), BF16),
+            pltpu.VMEM((64, LANES), BF16),
+            pltpu.VMEM((8, 8, 16, LANES), BF16),
+            *(pltpu.VMEM((16 * (64 >> i), LANES), F32) for i in range(3)),
             pltpu.SemaphoreType.REGULAR((2,)),
             dma((3,)),
             dma((2, BOX)),
@@ -406,6 +491,7 @@
             dma((2, 8)),
             dma((2,)),
             dma((2,)),
+            dma((2,)),
         ],
         compiler_params=pltpu.CompilerParams(
             collective_id=0, has_side_effects=True, vmem_limit_bytes=16 * 1024 * 1024
@@ -414,73 +500,33 @@
     )(*(pltpu.with_memory_space_constraint(a, pltpu.HBM) for a in (jnp.transpose(radiance, (0, 2, 1, 3)), cloud_weight, footprint.T)))
 
 
-GROUPS = ((0, 0, 0, 4), (0, 8, 4, 3), (1, 0, 7, 3))
-
-
-def pyramid_kernel(rows_ref, comp_a, comp_b, *refs):
-    outs, (composite, one, two, three, four, five), (t1, t2, t3), sems = refs[:6], refs[6:12], refs[12:15], refs[15]
-
-    def put(i):
-        return pltpu.make_async_copy(refs[6 + i], outs[i], sems.at[i])
-
-    before = lax.broadcasted_iota(jnp.int32, (LANES, LANES), 0)
-    after = lax.broadcasted_iota(jnp.int32, (LANES, LANES), 1)
-    same = (before >> 5) == (after >> 5)
-    mix = jnp.where(
-        jnp.logical_and(same, ((before & 31) >> 1) == (after & 31)), 0.25, 0.0
-    ).astype(BF16)
-    unit = jnp.where(before == after, 1.0, 0.0).astype(BF16)
-
-    def halve(values):
-        flat = values.reshape(-1, LANES)
-        return jnp.dot(flat, mix, preferred_element_type=F32).reshape(values.shape)
-
-    def keep(scratch, row, h, values):
-        for i in range(8):
-            at = row(i) * 24 + 16 * h
-            lines = 8 if h else 16
-            scratch[at : at + lines, :] = values[i].astype(F32)[0:lines]
-
-    def turn(scratch, out, height, width):
-        for r in range(24):
-            _, _, first, bands = GROUPS[r // 8]
-            lines = scratch[pl.ds(r, height, stride=24), :].astype(BF16)
-            turned = lax.dot_general(
-                unit[0 : 32 * bands], lines, (((1,), (1,)), ((), ())), preferred_element_type=F32
-            )
-            for g in range(bands):
-                out[r % 8, first + g] = turned[32 * g : 32 * g + width].astype(BF16)
-
-    level = [[rows_ref[h, xc] for xc in range(8)] for h in range(2)]
-    for h in range(2):
-        for xc in range(8):
-            keep(t1, lambda i, xc=xc: i * 8 + xc, h, level[h][xc])
-    turn(t1, one, 64, 32)
-    put(1).start()
+def pyramid_kernel(rows_b, one_a, two_a, three_a, fourth_a, comp_a, comp_b, *refs):
+    outs, (composite, four, five), parts, scratches, sems = refs[:6], refs[6:9], refs[9:12], refs[12:15], refs[15]
+    early = [
+        pltpu.make_async_copy(part, outs[1 + i].at[:, 0 : CHUNK[0][1]], sems.at[i]) for i, part in enumerate((one_a, two_a, three_a))
+    ]
+    late = [pltpu.make_async_copy(part, outs[1 + i].at[:, CHUNK[1][0] : BANDS], sems.at[3 + i]) for i, part in enumerate(parts)]
+    rest = [pltpu.make_async_copy(part, outs[i], sems.at[6 + k]) for k, (part, i) in enumerate(((composite, 0), (four, 4), (five, 5)))]
+    for copy in early:
+        copy.start()
     for comp, (first, end) in zip((comp_a, comp_b), CHUNK):
         lines = comp[...].astype(F32)[0 : 8 * (end - first)]
         composite[first:end] = lines.reshape(end - first, 8, LANES).astype(BF16)
-    put(0).start()
-    for scratch, out, m in ((t2, two, 4), (t3, three, 2), (None, None, 1)):
-        for h in range(2):
-            level[h] = [(halve(level[h][2 * q]) + halve(level[h][2 * q + 1])).astype(BF16) for q in range(m)]
-            if scratch is not None:
-                for q in range(m):
-                    keep(scratch, lambda i, q=q, m=m: i * m + q, h, level[h][q])
-        if scratch is not None:
-            turn(scratch, out, 8 * m, 4 * m)
-            put(2 if m == 4 else 3).start()
-    fourth, fifth = [], []
-    for h in range(2):
-        fourth.append(level[h][0].astype(F32))
-        last = halve(level[h][0]).reshape(4, 2, 16, LANES)
+    rest[0].start()
+
+    before, after, mix, unit = matrices()
+    level = [rows_b[i].astype(F32).reshape(8, 8, LANES) for i in range(8)]
+    fourth_b = overviews(1, level, mix, unit, scratches, parts, lambda depth: late[depth].start())
+    fourth, fifth = [fourth_a[...], fourth_b], []
+    for values in fourth:
+        last = halve(values, mix).reshape(4, 2, -1, LANES)
         fifth.append((last[:, 0] + last[:, 1]).astype(BF16).astype(F32))
 
     for values, out, height, width in ((fourth, four, 8, 4), (fifth, five, 4, 2)):
         columns = []
         for c in range(width):
             total = None
-            for h, line, first, bands in GROUPS:
+            for h, line, (first, bands) in ((0, 0, GROUPS[0][0]), (0, 8, GROUPS[0][1]), (1, 0, GROUPS[1][0])):
                 group = before >> 5
                 spread = jnp.where(
                     jnp.logical_and(
@@ -504,25 +550,26 @@
             for r in range(height):
                 at = 8 * (t * height + r)
                 out[t, r] = placed[at : at + width, 0:BANDS].astype(BF16)
-        put(4 if height == 8 else 5).start()
-    for i in range(6):
-        put(i).wait()
-
-
-def pyramid(rows, comp_a, comp_b):
+        rest[1 if height == 8 else 2].start()
+    for copy in early + late + rest:
+        copy.wait()
+
+
+def pyramid(*parts):
     vmem = pl.BlockSpec(memory_space=pltpu.VMEM)
     shapes = [(BANDS, 8, LANES)] + [(8, BANDS, 32 >> i, 64 >> i) for i in range(3)] + [(8, 8, 4, BANDS), (8, 4, 2, BANDS)]
     outs = pl.pallas_call(
         pyramid_kernel,
         out_shape=[jax.ShapeDtypeStruct(s, BF16) for s in shapes],
-        in_specs=[vmem] * 3,
+        in_specs=[vmem] * 7,
         out_specs=[pl.BlockSpec(memory_space=pl.ANY)] * 6,
-        scratch_shapes=[pltpu.VMEM(s, BF16) for s in shapes]
-        + [pltpu.VMEM((24 * (64 >> i), LANES), F32) for i in range(3)]
-        + [pltpu.SemaphoreType.DMA((6,))],
+        scratch_shapes=[pltpu.VMEM(shapes[i], BF16) for i in (0, 4, 5)]
+        + [pltpu.VMEM((8, BANDS - CHUNK[1][0], 32 >> i, 64 >> i), BF16) for i in range(3)]
+        + [pltpu.VMEM((8 * (64 >> i), LANES), F32) for i in range(3)]
+        + [pltpu.SemaphoreType.DMA((9,))],
         compiler_params=pltpu.CompilerParams(vmem_limit_bytes=16 * 1024 * 1024),
         name="pyramid",
-    )(rows, comp_a, comp_b)
+    )(*parts)
     orders = [(1, 0, 2)] + [(0, 1, 3, 2)] * 3 + [(0, 3, 1, 2)] * 2
     return tuple(jnp.transpose(out, order) for out, order in zip(outs, orders))
 

time: 66.3 us -> 64.3 us (0.970)
  Pallas kernels: 65.6 us -> 63.5 us
    pallas_call x1, Pallas kernels: 63.2 us -> 61.4 us  [exchange(): pl.pallas_call(exchange_kernel, out_shape=(jax.ShapeDtypeStruct((8, 64, L...]
where the time goes in v4:
time: 64.3 us; the launch traced here: 64.1 us
  Pallas kernels  63.5 us (99%)
    pallas_call x1, Pallas kernels, exchange(): pl.pallas_call(exchange_kernel, out_shape=(jax.ShapeDtypeStruct((8, 64, L...  61.4 us
    pallas_call x1, Pallas kernels, pyramid(): pl.pallas_call(pyramid_kernel, out_shape=[jax.ShapeDtypeStruct(s, BF16) f...  2.06 us

profile of v4, /device:TPU:1, one launch (start us, length us, event | category | flops | bytes accessed | tf_op | source)
XLA Modules:
  0.0 64.1 jit_solution(128171989328346065)
XLA Ops:
  0.6 61.4 %exchange.1 = (bf16[8,64,128]{2,1,0:T(8,128)(2,1)S(1)}, bf16[8,6,32,64]{3,2,1,0:T(8,128)(2,1)S(1)}, bf16[8,6,16,32]{3,2,1,0:T(8,128)(2,1)S(1)}, bf16[8,6,8,16]{3...) custom-call(bf16[1,10,8,8192]{3,2,1,0:T(8,128)(2,1)} %bitcast.8, ...), custom_call_target="tpu_custom_call" | custom-call | tf_op jit(solution)/shard_map/exchange/pallas_call | solution.py:458
  62.1 2.1 %pyramid.1 = (bf16[10,8,128]{2,1,0:T(8,128)(2,1)}, bf16[8,10,32,64]{3,2,1,0:T(8,128)(2,1)}, bf16[8,10,16,32]{3,2,1,0:T(8,128)(2,1)}, bf16[8,10,8,16]{3,2,1,0:T(8...) custom-call(bf16[8,64,128]{2,1,0:T(8,128)(2,1)S(1)} %get-tuple-element.19.rows_b, ...), custom_call_target="tpu_custom_call" | custom-call | tf_op jit(solution)/shard_map/pyramid/pallas_call | solution.py:561

commit v5 on v4

--- a/solution.py
+++ b/solution.py
@@ -326,12 +326,13 @@
         blank = jnp.zeros((8, LANES), F32)
         pixel = lax.broadcasted_iota(jnp.int32, (LANES, LANES), 0)
         spot = lax.broadcasted_iota(jnp.int32, (LANES, LANES), 1)
-        pooled = None
+        lefts, mixes = [], []
         for g in range(min(4, bands)):
-            left = jnp.concatenate([mean[g], mean[4 + g] if 4 + g < bands else blank], axis=0).astype(BF16)
-            mix = jnp.where(spot == 32 * g + ((pixel & 63) >> 1), 0.25, 0.0).astype(BF16)
-            part = jnp.dot(left, mix, preferred_element_type=F32)
-            pooled = part if pooled is None else pooled + part
+            lefts.append(jnp.concatenate([mean[g], mean[4 + g] if 4 + g < bands else blank], axis=0).astype(BF16))
+            mixes.append(jnp.where(spot == 32 * g + ((pixel & 63) >> 1), 0.25, 0.0).astype(BF16))
+        pooled = jnp.dot(
+            jnp.concatenate(lefts, axis=1), jnp.concatenate(mixes, axis=0), preferred_element_type=F32
+        )
         pool[h] = pooled.astype(BF16)
 
         def send_line(z2, _):
@@ -390,15 +391,41 @@
         lax.fori_loop(1, 8, send_plane, 0)
         rows[h][xc] = whole_line[h][...]
 
-    reduce_box(0)
-    reduce_box(1)
-    scale = finish_mean(0, None)
-    finish_mean(1, scale)
-    spread_line(0)
-    spread_line(1)
-
-    for h in range(2):
-        def wait_plane(i, _, h=h):
+    def drain_box(h):
+        def drain(slot, same):
+            box_copy(h, same, slot, other_core).wait_send()
+
+        each_pair(0, BOX - 1, drain)
+
+    def drain_ring(h):
+        def drain(i, _):
+            ring_copy(h, i).wait_send()
+            return 0
+
+        lax.fori_loop(1, 8, drain, 0)
+
+    def drain_line(h):
+        @pl.when(jnp.logical_not(stays(my_row)))
+        def _():
+            comp_copy(h).wait_send()
+
+        @pl.when(jnp.logical_not(jnp.logical_and(at_home, my_row == z_lo)))
+        def _():
+            pltpu.make_async_remote_copy(
+                src_ref=means[h], dst_ref=comp[h], send_sem=sc_sem.at[h], recv_sem=rc_sem.at[h],
+                device_id=maker_device(z_lo), device_id_type=MESH,
+            ).wait_recv()
+
+        def drain(z2, _):
+            @pl.when(jnp.logical_not(stays(z2)))
+            def _():
+                line_copy(h, z2).wait_send()
+            return 0
+
+        lax.fori_loop(0, 8, drain, 0)
+
+    def wait_plane(h):
+        def wait(i, _):
             xc2, device = plane_device(i)
             pltpu.make_async_remote_copy(
                 src_ref=whole_line[h], dst_ref=rows[h].at[xc2], send_sem=sg2_sem.at[h, i], recv_sem=rg2_sem.at[h, xc2],
@@ -406,49 +433,35 @@
             ).wait_recv()
             return 0
 
-        lax.fori_loop(1, 8, wait_plane, 0)
-        if h == 0:
-            _, _, mix, unit = matrices()
-            level = [rows_a[i].astype(F32) for i in range(8)]
-            fourth[...] = overviews(0, level, mix, unit, (t1, t2, t3), (one, two, three), lambda depth: None)
-
+        lax.fori_loop(1, 8, wait, 0)
+
+    def drain_plane(h):
+        def drain(i, _):
+            plane_copy(h, i).wait_send()
+            return 0
+
+        lax.fori_loop(1, 8, drain, 0)
+
+    reduce_box(0)
+    drain_box(0)
+    reduce_box(1)
+    drain_box(1)
+    scale = finish_mean(0, None)
+    drain_ring(0)
+    finish_mean(1, scale)
+    drain_ring(1)
     swap_copy().wait_send()
+    spread_line(0)
+    spread_line(1)
+    wait_plane(0)
+    _, _, mix, unit = matrices()
+    level = [rows_a[i].astype(F32) for i in range(8)]
+    fourth[...] = overviews(0, level, mix, unit, (t1, t2, t3), (one, two, three), lambda depth: None)
     for h in range(2):
-        def drain_box(slot, same, h=h):
-            box_copy(h, same, slot, other_core).wait_send()
-
-        each_pair(0, BOX - 1, drain_box)
-
-        def drain_ring(i, _, h=h):
-            ring_copy(h, i).wait_send()
-            return 0
-
-        lax.fori_loop(1, 8, drain_ring, 0)
-
-        @pl.when(jnp.logical_not(stays(my_row)))
-        def _(h=h):
-            comp_copy(h).wait_send()
-
-        @pl.when(jnp.logical_not(jnp.logical_and(at_home, my_row == z_lo)))
-        def _(h=h):
-            pltpu.make_async_remote_copy(
-                src_ref=means[h], dst_ref=comp[h], send_sem=sc_sem.at[h], recv_sem=rc_sem.at[h],
-                device_id=maker_device(z_lo), device_id_type=MESH,
-            ).wait_recv()
-
-        def drain_line(z2, _, h=h):
-            @pl.when(jnp.logical_not(stays(z2)))
-            def _():
-                line_copy(h, z2).wait_send()
-            return 0
-
-        lax.fori_loop(0, 8, drain_line, 0)
-
-        def drain_rows(i, _, h=h):
-            plane_copy(h, i).wait_send()
-            return 0
-
-        lax.fori_loop(1, 8, drain_rows, 0)
+        drain_line(h)
+    drain_plane(0)
+    wait_plane(1)
+    drain_plane(1)
 
 
 def exchange(radiance, cloud_weight, footprint):
@@ -516,7 +529,9 @@
 
     before, after, mix, unit = matrices()
     level = [rows_b[i].astype(F32).reshape(8, 8, LANES) for i in range(8)]
-    fourth_b = overviews(1, level, mix, unit, scratches, parts, lambda depth: late[depth].start())
+    fourth_b = overviews(1, level, mix, unit, scratches, parts, lambda depth: None)
+    for copy in late:
+        copy.start()
     fourth, fifth = [fourth_a[...], fourth_b], []
     for values in fourth:
         last = halve(values, mix).reshape(4, 2, -1, LANES)

time: 64.3 us -> 63.3 us (0.984)
  Pallas kernels: 63.5 us -> 62.6 us
    pallas_call x1, Pallas kernels: 61.4 us -> 60.5 us  [exchange(): pl.pallas_call(exchange_kernel, out_shape=(jax.ShapeDtypeStruct((8, 64, L...]
where the time goes in v5:
time: 63.3 us; the launch traced here: 63.2 us
  Pallas kernels  62.6 us (99%)
  between operations  0.64 us (1%)
    pallas_call x1, Pallas kernels, exchange(): pl.pallas_call(exchange_kernel, out_shape=(jax.ShapeDtypeStruct((8, 64, L...  60.5 us
    pallas_call x1, Pallas kernels, pyramid(): pl.pallas_call(pyramid_kernel, out_shape=[jax.ShapeDtypeStruct(s, BF16) f...  2.03 us

profile of v5, /device:TPU:1, one launch (start us, length us, event | category | flops | bytes accessed | tf_op | source)
XLA Modules:
  0.0 63.2 jit_solution(6644184273998423666)
XLA Ops:
  0.6 60.5 %exchange.1 = (bf16[8,64,128]{2,1,0:T(8,128)(2,1)S(1)}, bf16[8,6,32,64]{3,2,1,0:T(8,128)(2,1)S(1)}, bf16[8,6,16,32]{3,2,1,0:T(8,128)(2,1)S(1)}, bf16[8,6,8,16]{3...) custom-call(bf16[1,10,8,8192]{3,2,1,0:T(8,128)(2,1)} %bitcast.8, ...), custom_call_target="tpu_custom_call" | custom-call | tf_op jit(solution)/shard_map/exchange/pallas_call | solution.py:471
  61.2 2.0 %pyramid.1 = (bf16[10,8,128]{2,1,0:T(8,128)(2,1)}, bf16[8,10,32,64]{3,2,1,0:T(8,128)(2,1)}, bf16[8,10,16,32]{3,2,1,0:T(8,128)(2,1)}, bf16[8,10,8,16]{3,2,1,0:T(8...) custom-call(bf16[8,64,128]{2,1,0:T(8,128)(2,1)S(1)} %get-tuple-element.19.rows_b, ...), custom_call_target="tpu_custom_call" | custom-call | tf_op jit(solution)/shard_map/pyramid/pallas_call | solution.py:576

commit v6 on v5

--- a/solution.py
+++ b/solution.py
@@ -70,6 +70,37 @@
         done(depth)
 
 
+def fifth_of(fourth, mix):
+    last = halve(fourth, mix).reshape(4, 2, -1, LANES)
+    return (last[:, 0] + last[:, 1]).astype(BF16).astype(F32)
+
+
+def bands_to_lanes(values, groups, height, width):
+    before, after, _, _ = matrices()
+    group = before >> 5
+    columns = []
+    for c in range(width):
+        total = None
+        for k, (first, bands) in enumerate(groups):
+            spread = jnp.where(
+                jnp.logical_and(jnp.logical_and((before & 31) == c, after == first + group), group < bands), 1.0, 0.0
+            ).astype(BF16)
+            left = values[:, 8 * k : 8 * k + 8, :].reshape(8 * height, LANES).astype(BF16)
+            part = jnp.dot(left, spread, preferred_element_type=F32)
+            total = part if total is None else total + part
+        columns.append(total)
+    return jnp.concatenate(columns, axis=0)
+
+
+def row_order(height, width):
+    shape = (64 * height, 8 * height * width)
+    to = lax.broadcasted_iota(jnp.int32, shape, 0)
+    of = lax.broadcasted_iota(jnp.int32, shape, 1)
+    high = {8: 3, 4: 2}[height]
+    t, r, c = to >> (3 + high), (to >> 3) & (height - 1), to & 7
+    return jnp.where(of == c * (8 * height) + r * 8 + t, 1.0, 0.0).astype(BF16)
+
+
 def position():
     scene = lax.axis_index("scene")
     tile = lax.axis_index("tile")
@@ -82,7 +113,7 @@
 
 
 def exchange_kernel(
-    rad_ref, weight_ref, foot_ref, rows_b, one, two, three, fourth, comp_a, comp_b,
+    rad_ref, weight_ref, foot_ref, rows_b, one, two, three, lanes_4, lanes_5, order_4, order_5, comp_a, comp_b,
     rad, weight, foot, send_a, send_b, recv_a, recv_b, assign, acc, send3_a, send3_b, recv3_a, recv3_b, mean_a, mean_b, pool, swap_out, swap_in, line, packed, rows_a, t1, t2, t3,
     ring_sem, in_sem, send_sem, recv_sem, send3_sem, recv3_sem, sg1_sem, rg1_sem, sg2_sem, rg2_sem, sc_sem, rc_sem, swap_sem,
 ):
@@ -234,6 +265,8 @@
     target = jnp.sum(jnp.where(own, named, 0.0), axis=0, keepdims=True).astype(jnp.int32) + ((lane & 8) << 3)
     row = lax.broadcasted_iota(jnp.int32, (128, 16 * BOX), 0)
     assign[...] = jnp.where(row == target, 1.0, 0.0).astype(BF16)
+    order_4[...] = row_order(8, 4)
+    order_5[...] = row_order(4, 2)
     hear_ring()
     tell_ring()
 
@@ -456,7 +489,9 @@
     wait_plane(0)
     _, _, mix, unit = matrices()
     level = [rows_a[i].astype(F32) for i in range(8)]
-    fourth[...] = overviews(0, level, mix, unit, (t1, t2, t3), (one, two, three), lambda depth: None)
+    fourth = overviews(0, level, mix, unit, (t1, t2, t3), (one, two, three), lambda depth: None)
+    lanes_4[...] = bands_to_lanes(fourth, GROUPS[0], 8, 4)
+    lanes_5[...] = bands_to_lanes(fifth_of(fourth, mix), GROUPS[0], 4, 2)
     for h in range(2):
         drain_line(h)
     drain_plane(0)
@@ -473,11 +508,14 @@
         out_shape=(
             jax.ShapeDtypeStruct((8, 64, LANES), BF16),
             *(jax.ShapeDtypeStruct((8, CHUNK[0][1], 32 >> i, 64 >> i), BF16) for i in range(3)),
-            jax.ShapeDtypeStruct((8, 16, LANES), F32),
+            jax.ShapeDtypeStruct((256, LANES), F32),
+            jax.ShapeDtypeStruct((64, LANES), F32),
+            jax.ShapeDtypeStruct((512, 256), BF16),
+            jax.ShapeDtypeStruct((256, 64), BF16),
             *(jax.ShapeDtypeStruct((rows, LANES), BF16) for rows in ROWS),
         ),
         in_specs=[any_space] * 3,
-        out_specs=(vmem,) * 7,
+        out_specs=(vmem,) * 10,
         scratch_shapes=[
             pltpu.VMEM((BANDS, K, PIX), BF16),
             pltpu.VMEM((K, PIX), jnp.int32),
@@ -513,7 +551,7 @@
     )(*(pltpu.with_memory_space_constraint(a, pltpu.HBM) for a in (jnp.transpose(radiance, (0, 2, 1, 3)), cloud_weight, footprint.T)))
 
 
-def pyramid_kernel(rows_b, one_a, two_a, three_a, fourth_a, comp_a, comp_b, *refs):
+def pyramid_kernel(rows_b, one_a, two_a, three_a, lanes_4, lanes_5, order_4, order_5, comp_a, comp_b, *refs):
     outs, (composite, four, five), parts, scratches, sems = refs[:6], refs[6:9], refs[9:12], refs[12:15], refs[15]
     early = [
         pltpu.make_async_copy(part, outs[1 + i].at[:, 0 : CHUNK[0][1]], sems.at[i]) for i, part in enumerate((one_a, two_a, three_a))
@@ -527,40 +565,18 @@
         composite[first:end] = lines.reshape(end - first, 8, LANES).astype(BF16)
     rest[0].start()
 
-    before, after, mix, unit = matrices()
+    _, _, mix, unit = matrices()
     level = [rows_b[i].astype(F32).reshape(8, 8, LANES) for i in range(8)]
     fourth_b = overviews(1, level, mix, unit, scratches, parts, lambda depth: None)
     for copy in late:
         copy.start()
-    fourth, fifth = [fourth_a[...], fourth_b], []
-    for values in fourth:
-        last = halve(values, mix).reshape(4, 2, -1, LANES)
-        fifth.append((last[:, 0] + last[:, 1]).astype(BF16).astype(F32))
-
-    for values, out, height, width in ((fourth, four, 8, 4), (fifth, five, 4, 2)):
-        columns = []
-        for c in range(width):
-            total = None
-            for h, line, (first, bands) in ((0, 0, GROUPS[0][0]), (0, 8, GROUPS[0][1]), (1, 0, GROUPS[1][0])):
-                group = before >> 5
-                spread = jnp.where(
-                    jnp.logical_and(
-                        jnp.logical_and((before & 31) == c, after == first + group), group < bands
-                    ),
-                    1.0, 0.0,
-                ).astype(BF16)
-                left = values[h][:, line : line + 8, :].reshape(8 * height, LANES).astype(BF16)
-                part = jnp.dot(left, spread, preferred_element_type=F32)
-                total = part if total is None else total + part
-            columns.append(total)
-        stacked = jnp.concatenate(columns, axis=0).astype(BF16)
-        shape = (64 * height, 8 * height * width)
-        to = lax.broadcasted_iota(jnp.int32, shape, 0)
-        of = lax.broadcasted_iota(jnp.int32, shape, 1)
-        high = {8: 3, 4: 2}[height]
-        t, r, c = to >> (3 + high), (to >> 3) & (height - 1), to & 7
-        order = jnp.where(of == c * (8 * height) + r * 8 + t, 1.0, 0.0).astype(BF16)
-        placed = jnp.dot(order, stacked, preferred_element_type=F32)
+    fifth_b = fifth_of(fourth_b, mix)
+
+    for values, lanes, order, out, height, width in (
+        (fourth_b, lanes_4, order_4, four, 8, 4), (fifth_b, lanes_5, order_5, five, 4, 2)
+    ):
+        stacked = (lanes[...] + bands_to_lanes(values, GROUPS[1], height, width)).astype(BF16)
+        placed = jnp.dot(order[...], stacked, preferred_element_type=F32)
         for t in range(8):
             for r in range(height):
                 at = 8 * (t * height + r)
@@ -576,7 +592,7 @@
     outs = pl.pallas_call(
         pyramid_kernel,
         out_shape=[jax.ShapeDtypeStruct(s, BF16) for s in shapes],
-        in_specs=[vmem] * 7,
+        in_specs=[vmem] * 10,
         out_specs=[pl.BlockSpec(memory_space=pl.ANY)] * 6,
         scratch_shapes=[pltpu.VMEM(shapes[i], BF16) for i in (0, 4, 5)]
         + [pltpu.VMEM((8, BANDS - CHUNK[1][0], 32 >> i, 64 >> i), BF16) for i in range(3)]

time: 63.3 us -> 63.5 us (level)
  no operation moved by 1% of the time
where the time goes in v6:
time: 63.5 us; the launch traced here: 63.3 us
  Pallas kernels  62.7 us (99%)
  between operations  0.64 us (1%)
    pallas_call x1, Pallas kernels, exchange(): pl.pallas_call(exchange_kernel, out_shape=(jax.ShapeDtypeStruct((8, 64, L...  60.7 us
    pallas_call x1, Pallas kernels, pyramid(): pl.pallas_call(pyramid_kernel, out_shape=[jax.ShapeDtypeStruct(s, BF16) f...  2.03 us

profile of v6, /device:TPU:1, one launch (start us, length us, event | category | flops | bytes accessed | tf_op | source)
XLA Modules:
  0.0 63.3 jit_solution(16135641120708762881)
XLA Ops:
  0.6 60.7 %exchange.1 = (bf16[8,64,128]{2,1,0:T(8,128)(2,1)S(1)}, bf16[8,6,32,64]{3,2,1,0:T(8,128)(2,1)S(1)}, bf16[8,6,16,32]{3,2,1,0:T(8,128)(2,1)S(1)}, bf16[8,6,8,16]{3...) custom-call(bf16[1,10,8,8192]{3,2,1,0:T(8,128)(2,1)} %bitcast.8, ...), custom_call_target="tpu_custom_call" | custom-call | tf_op jit(solution)/shard_map/exchange/pallas_call | solution.py:506
  61.3 2.0 %pyramid.1 = (bf16[10,8,128]{2,1,0:T(8,128)(2,1)}, bf16[8,10,32,64]{3,2,1,0:T(8,128)(2,1)}, bf16[8,10,16,32]{3,2,1,0:T(8,128)(2,1)}, bf16[8,10,8,16]{3,2,1,0:T(8...) custom-call(bf16[8,64,128]{2,1,0:T(8,128)(2,1)S(1)} %get-tuple-element.22.rows_b, ...), custom_call_target="tpu_custom_call" | custom-call | tf_op jit(solution)/shard_map/pyramid/pallas_call | solution.py:592

commit v7 on v5

--- a/solution.py
+++ b/solution.py
@@ -271,7 +271,7 @@
             hear_ring()
 
         def send_ring(i, _):
-            ring_copy(h, i).start()
+            ring_copy(h, 4 + lax.div(i, 2) * (1 - 2 * lax.rem(i, 2))).start()
             return 0
 
         lax.fori_loop(1, 8, send_ring, 0)

time: 63.3 us -> 63.1 us (level)
  no operation moved by 1% of the time
where the time goes in v7:
time: 63.1 us; the launch traced here: 63 us
  Pallas kernels  62.3 us (99%)
  between operations  0.64 us (1%)
    pallas_call x1, Pallas kernels, exchange(): pl.pallas_call(exchange_kernel, out_shape=(jax.ShapeDtypeStruct((8, 64, L...  60.3 us
    pallas_call x1, Pallas kernels, pyramid(): pl.pallas_call(pyramid_kernel, out_shape=[jax.ShapeDtypeStruct(s, BF16) f...  2.04 us

profile of v7, /device:TPU:1, one launch (start us, length us, event | category | flops | bytes accessed | tf_op | source)
XLA Modules:
  0.0 63.0 jit_solution(8097674774492819023)
XLA Ops:
  0.6 60.3 %exchange.1 = (bf16[8,64,128]{2,1,0:T(8,128)(2,1)S(1)}, bf16[8,6,32,64]{3,2,1,0:T(8,128)(2,1)S(1)}, bf16[8,6,16,32]{3,2,1,0:T(8,128)(2,1)S(1)}, bf16[8,6,8,16]{3...) custom-call(bf16[1,10,8,8192]{3,2,1,0:T(8,128)(2,1)} %bitcast.8, ...), custom_call_target="tpu_custom_call" | custom-call | tf_op jit(solution)/shard_map/exchange/pallas_call | solution.py:471
  60.9 2.0 %pyramid.1 = (bf16[10,8,128]{2,1,0:T(8,128)(2,1)}, bf16[8,10,32,64]{3,2,1,0:T(8,128)(2,1)}, bf16[8,10,16,32]{3,2,1,0:T(8,128)(2,1)}, bf16[8,10,8,16]{3,2,1,0:T(8...) custom-call(bf16[8,64,128]{2,1,0:T(8,128)(2,1)S(1)} %get-tuple-element.19.rows_b, ...), custom_call_target="tpu_custom_call" | custom-call | tf_op jit(solution)/shard_map/pyramid/pallas_call | solution.py:576

commit v8 on v7

--- a/solution.py
+++ b/solution.py
@@ -385,7 +385,7 @@
                 packed[16 * q : 16 * q + 16, :] = jnp.concatenate(both, axis=0).astype(BF16)
 
         def send_plane(i, _):
-            plane_copy(h, i).start()
+            plane_copy(h, 4 + lax.div(i, 2) * (1 - 2 * lax.rem(i, 2))).start()
             return 0
 
         lax.fori_loop(1, 8, send_plane, 0)

time: 63.1 us -> 62.5 us (level)
  no operation moved by 1% of the time
where the time goes in v8:
time: 62.5 us; the launch traced here: 62.3 us
  Pallas kernels  61.7 us (99%)
  between operations  0.64 us (1%)
    pallas_call x1, Pallas kernels, exchange(): pl.pallas_call(exchange_kernel, out_shape=(jax.ShapeDtypeStruct((8, 64, L...  59.7 us
    pallas_call x1, Pallas kernels, pyramid(): pl.pallas_call(pyramid_kernel, out_shape=[jax.ShapeDtypeStruct(s, BF16) f...  2.04 us

profile of v8, /device:TPU:1, one launch (start us, length us, event | category | flops | bytes accessed | tf_op | source)
XLA Modules:
  0.0 62.3 jit_solution(17901902287329807319)
XLA Ops:
  0.6 59.7 %exchange.1 = (bf16[8,64,128]{2,1,0:T(8,128)(2,1)S(1)}, bf16[8,6,32,64]{3,2,1,0:T(8,128)(2,1)S(1)}, bf16[8,6,16,32]{3,2,1,0:T(8,128)(2,1)S(1)}, bf16[8,6,8,16]{3...) custom-call(bf16[1,10,8,8192]{3,2,1,0:T(8,128)(2,1)} %bitcast.8, ...), custom_call_target="tpu_custom_call" | custom-call | tf_op jit(solution)/shard_map/exchange/pallas_call | solution.py:471
  60.3 2.0 %pyramid.1 = (bf16[10,8,128]{2,1,0:T(8,128)(2,1)}, bf16[8,10,32,64]{3,2,1,0:T(8,128)(2,1)}, bf16[8,10,16,32]{3,2,1,0:T(8,128)(2,1)}, bf16[8,10,8,16]{3,2,1,0:T(8...) custom-call(bf16[8,64,128]{2,1,0:T(8,128)(2,1)S(1)} %get-tuple-element.19.rows_b, ...), custom_call_target="tpu_custom_call" | custom-call | tf_op jit(solution)/shard_map/pyramid/pallas_call | solution.py:576
